TPU v7x, 32 devices: a whole 2x2x4 slice. The times are simulated.
32 devices in a mesh: dp: 8 (over z, y), mp: 4 (over x, core).
Axes of the slice: x: 2, y: 2, z: 4, core: 2. Of those that a mesh axis runs over, the one named last changes fastest.
Arguments:
- decoder_rows: bfloat16 [16384, 768], P(('dp', 'mp')), may hold values from -6 to 6
- memory_rows: bfloat16 [49152, 768], P(('dp', 'mp')), may hold values from -6 to 6
- decoder_token_length: int32 [32], P('dp'), may hold values from 1 to 512, 12288 in all
- memory_length: int32 [32], P('dp'), may hold values from 1 to 1536, 36864 in all
- bucket_ids: int32 [512, 512], replicated, may hold values from 0 to 31
- relative_bucket_bias: bfloat16 [32, 12], P(None, 'mp'), may hold values from -4 to 4
- self_gain: bfloat16 [768], replicated, may hold values from 0.5 to 1.5
- self_query: bfloat16 [768, 768], P(None, 'mp'), may hold values from -0.21875 to 0.21875
- self_key: bfloat16 [768, 768], P(None, 'mp'), may hold values from -0.21875 to 0.21875
- self_value: bfloat16 [768, 768], P(None, 'mp'), may hold values from -0.21875 to 0.21875
- self_out: bfloat16 [768, 768], P('mp'), may hold values from -1.25 to 1.25
- cross_gain: bfloat16 [768], replicated, may hold values from 0.5 to 1.5
- cross_query: bfloat16 [768, 768], P(None, 'mp'), may hold values from -0.21875 to 0.21875
- cross_key: bfloat16 [768, 768], P(None, 'mp'), may hold values from -0.21875 to 0.21875
- cross_value: bfloat16 [768, 768], P(None, 'mp'), may hold values from -0.21875 to 0.21875
- cross_out: bfloat16 [768, 768], P('mp'), may hold values from -1.75 to 1.75
- hidden_gain: bfloat16 [768], replicated, may hold values from 0.5 to 1.5
- widen_weight: bfloat16 [768, 3072], P(None, 'mp'), may hold values from -0.21875 to 0.21875
- narrow_weight: bfloat16 [3072, 768], P('mp'), may hold values from -0.109375 to 0.109375
- layer_cotangent: bfloat16 [16384, 768], P(('dp', 'mp')), may hold values from -6 to 6
Outputs:
- layer_output: bfloat16 [16384, 768], P(('dp', 'mp'))
- input_grad: float32 [16384, 768], P(('dp', 'mp'))
- memory_grad: bfloat16 [49152, 768], P(('dp', 'mp'))
- position_grad: float32 [32, 12], P(None, 'mp')
- self_gain_grad: float32 [768], replicated
- self_query_grad: float32 [768, 768], P(None, 'mp')
- self_key_grad: float32 [768, 768], P(None, 'mp')
- self_value_grad: float32 [768, 768], P(None, 'mp')
- self_out_grad: float32 [768, 768], P('mp')
- cross_gain_grad: float32 [768], replicated
- cross_query_grad: float32 [768, 768], P(None, 'mp')
- cross_key_grad: float32 [768, 768], P(None, 'mp')
- cross_value_grad: float32 [768, 768], P(None, 'mp')
- cross_out_grad: float32 [768, 768], P('mp')
- hidden_gain_grad: float32 [768], replicated
- widen_grad: float32 [768, 3072], P(None, 'mp')
- narrow_grad: float32 [3072, 768], P('mp')
Inputs may be any that keep to these rules, and one draw needn't show every extreme that they name: decoder_token_length[j] counts document j's real decoder tokens; some document has 512. memory_length[j] counts document j's real memory tokens; some document has 1536.
All inputs are finite; a program needn't handle non-finite values. No bound on the sum of `decoder_token_length` or of `memory_length` on one device may be relied on, other than what follows from the above.
Results may differ from a plain program's by a relative error of at most 0.024.
Values may be sent and summed in bfloat16 or wider, within the bound.
A program may use at most 192 MiB of HBM per device.

v0:
```python
import functools

import jax
import jax.numpy as jnp
from jax import lax
from jax.experimental import pallas as pl
from jax.experimental.pallas import tpu as pltpu
from jax.sharding import PartitionSpec as P

HEAD_DIM = 64
NORM_EPS = 1e-06
MASKED = -1e30
SCALE = HEAD_DIM**-0.5
BF16 = jnp.bfloat16
F32 = jnp.float32
LANES = 128
TABLE_ROWS = 16
TILE_ROWS = 16
LARGEST_SUM = 1e30
LATE_STEP = 4
HEAD_BLOCK = 256
BLOCK_HEADS = HEAD_BLOCK // HEAD_DIM
Q_BLOCK = 256
K_BLOCK = 512
FORWARD_K_BLOCK = 256
HIDDEN_BLOCK = 256
MEMORY_BLOCK = 768
FINISH_BLOCK = 384
ROW_BLOCK = 128
VMEM_BYTES = 56 * 1024 * 1024
GELU_ROOT = 0.7978845608028654
GELU_CUBE = 0.044715


def dot_nn(a, b):
    return lax.dot_general(a, b, (((1,), (0,)), ((), ())), preferred_element_type=F32)


def dot_nt(a, b):
    return lax.dot_general(a, b, (((1,), (1,)), ((), ())), preferred_element_type=F32)


def dot_tn(a, b):
    return lax.dot_general(a, b, (((0,), (0,)), ((), ())), preferred_element_type=F32)


def flip(a):
    return a.astype(F32).T.astype(BF16)


def spans(size, step):
    return [slice(i, i + step) for i in range(0, size, step)]


def norm_scale(rows):
    return lax.rsqrt(jnp.mean(rows * rows, axis=-1, keepdims=True) + NORM_EPS)


def norm_into(normed_ref, rows_ref, gain_ref):
    for span in spans(rows_ref.shape[0], ROW_BLOCK):
        rows = rows_ref[span].astype(F32)
        normed_ref[span] = (rows * norm_scale(rows) * gain_ref[...]).astype(BF16)


def norm_back_into(span, grad, out_ref, low_ref, gain_grad_ref, rows_ref, gain_ref, add_ref):
    rows = rows_ref[span].astype(F32)
    scale = norm_scale(rows)
    unit = rows * scale
    grad_unit = grad * gain_ref[...]
    mean = jnp.mean(grad_unit * unit, axis=-1, keepdims=True)
    out = add_ref[span].astype(F32) + scale * (grad_unit - unit * mean)
    out_ref[span] = out
    if low_ref is not None:
        low_ref[span] = out.astype(BF16)
    gain_grad_ref[...] += jnp.sum((grad * unit).reshape(-1, 8, rows.shape[1]), axis=0)


def gelu_and_slope(v):
    square = v * v
    bend = jnp.tanh(GELU_ROOT * (v + GELU_CUBE * v * square))
    half = 0.5 * (1.0 + bend)
    slope = half + 0.5 * v * (1.0 - bend * bend) * GELU_ROOT * (1.0 + 3.0 * GELU_CUBE * square)
    return v * half, slope


def lane_block(start):
    return pl.ds(pl.multiple_of(start, LANES), LANES)


def extra_lanes(rows, allowed):
    lane = lax.broadcasted_iota(jnp.int32, (rows, LANES), 1) % HEAD_DIM
    first = MASKED if allowed is None else jnp.where(allowed, 0.0, MASKED)
    return jnp.where(lane == 0, first, jnp.where(lane < 4, 1.0, 0.0)).astype(BF16)


def pick(which, block, other):
    lane = lax.broadcasted_iota(jnp.int32, block.shape, 1)
    return jnp.where((lane < HEAD_DIM) == (which == 0), block, other)


def half_rows(which):
    return slice(which * HEAD_DIM, (which + 1) * HEAD_DIM)


def split(values):
    high = values.astype(BF16).astype(F32)
    rest = values - high
    middle = rest.astype(BF16).astype(F32)
    return high, middle, rest - middle


def with_extra(which, block_t, masked, minus):
    columns = block_t.shape[1]
    row = lax.broadcasted_iota(jnp.int32, (HEAD_DIM, columns), 0)
    extra = jnp.where(row == 0, 1.0 if masked else 0.0, 0.0)
    if minus is not None:
        for i, part in enumerate(split(minus)):
            extra = jnp.where(row == i + 1, -part, extra)
    own = block_t[half_rows(which)]
    return jnp.concatenate([own, extra] if which == 0 else [extra, own], axis=0).astype(BF16)


def bias_block(table_ref, ids_ref, index, rows, start):
    row = jnp.broadcast_to(table_ref[pl.ds(index, 1), :], (rows, LANES))
    return jnp.concatenate(
        [
            jnp.take_along_axis(row, ids_ref[:rows, c : c + LANES], axis=1)
            for c in range(start, start + Q_BLOCK, LANES)
        ],
        axis=1,
    )


def ring_place(me, size):
    return jnp.where(me % 2 == 0, me // 2, size - 1 - me // 2)


def ring_device(place, size):
    return jnp.where(place < size // 2, 2 * place, 2 * (size - 1 - place) + 1)


def ring_ways(size):
    me = lax.axis_index("dp")
    place = ring_place(me, size)
    return (
        (place, ring_device((place + 1) % size, size)),
        (size - 1 - place, ring_device((place + size - 1) % size, size)),
    )


def differing(row, bit):
    return row + bit - 2 * bit * ((row // bit) % 2)


def remote(source, target, send_sem, recv_sem, device):
    return pltpu.make_async_remote_copy(
        src_ref=source,
        dst_ref=target,
        send_sem=send_sem,
        recv_sem=recv_sem,
        device_id=device,
        device_id_type=pl.DeviceIdType.MESH,
    )


def greet(bits, devices=()):
    me, row = lax.axis_index("dp"), lax.axis_index("mp")
    barrier = pltpu.get_barrier_semaphore()
    others = [(me, differing(row, bit)) for bit in bits] + [(device, row) for device in devices]
    for other in others:
        pl.semaphore_signal(
            barrier, inc=1, device_id=other, device_id_type=pl.DeviceIdType.MESH
        )
    pl.semaphore_wait(barrier, len(others))


def to_differing(bit, source, target, sems):
    me, row = lax.axis_index("dp"), lax.axis_index("mp")
    return remote(source, target, sems.at[0], sems.at[1], (me, differing(row, bit)))


class Scatter:
    def __init__(self, size, part, slots, done, send, came):
        self.size, self.part, self.slots, self.done = size, part, slots, done
        self.send, self.came = send, came
        self.ways, self.row = ring_ways(size), lax.axis_index("mp")

    def span(self, way, number):
        rows = self.slots.shape[3]
        return pl.ds(pl.multiple_of((way * self.size + number) * rows, 16), rows)

    def copy(self, way, step, source):
        return remote(
            source,
            self.slots.at[way, step],
            self.send.at[way, step],
            self.came.at[way, step],
            (self.ways[way][1], self.row),
        )

    def first(self, way):
        return self.copy(way, 0, self.part.at[:, self.span(way, self.ways[way][0])])

    def next(self, way, step):
        return self.copy(way, step, self.slots.at[way, step - 1])

    def begin(self):
        for way in range(2):
            self.first(way).start()

    def total(self, way, step):
        self.copy(way, step, self.slots.at[way, step]).wait_recv()
        span = self.span(way, (self.ways[way][0] - step - 1 + self.size) % self.size)
        return low_sum(self.slots[way, step], self.part[:, span])

    def advance(self, step):
        for way in range(2):
            self.slots[way, step - 1] = self.total(way, step - 1)
            self.next(way, step).start()

    def turn(self):
        for way in range(2):
            self.done[way] = self.total(way, self.size - 2)

    def wait_sent(self):
        for way in range(2):
            self.first(way).wait_send()

        def sent(step, carry):
            for way in range(2):
                self.next(way, step).wait_send()
            return carry

        lax.fori_loop(1, self.size - 1, sent, 0)


def low_sum(a, b):
    return (a.astype(F32) + b.astype(F32)).astype(BF16)


class Stack:
    def __init__(self, sources, stack_ref, sems, kinds, rows):
        features = stack_ref.shape[0] // kinds
        self.copies = [
            [
                pltpu.make_async_copy(
                    source.at[pl.ds(kind * rows, rows)],
                    stack_ref.at[pl.ds(kind * features + p * rows, rows)],
                    sems.at[p, kind],
                )
                for p, source in enumerate(sources)
            ]
            for kind in range(kinds)
        ]

    def start(self):
        for copies in self.copies:
            for copy in copies:
                copy.start()

    def wait(self, *kinds):
        for kind in kinds:
            for copy in self.copies[kind]:
                copy.wait()


def table_copies(sources, tables_ref, sems, kinds):
    start = sources[0].shape[0] - TABLE_ROWS
    return [
        pltpu.make_async_copy(
            source.at[pl.ds(start, TABLE_ROWS)], tables_ref.at[p], sems.at[p, kinds]
        )
        for p, source in enumerate(sources)
    ]


def table_into(table_ref, tables_ref, heads, buckets):
    for p in range(tables_ref.shape[0]):
        rows = tables_ref[p, :, :LANES].astype(F32)
        lane = lax.broadcasted_iota(jnp.int32, rows.shape, 1)
        rows = jnp.where(lane < buckets, rows, MASKED)
        for h in range(heads):
            table_ref[p * heads + h : p * heads + h + 1, :] = rows[h : h + 1, :]


def self_forward_kernel(heads, buckets, shares, rows_ref, gain_ref, ids_ref, *refs):
    sources = refs[:shares]
    q_ref, k_ref, v_ref, mixed_ref, lse_ref, bias_ref, out_ref = refs[shares : shares + 7]
    w_ref, tables_ref, table_ref, normed_ref, sems = refs[shares + 7 :]
    step = pl.program_id(0)
    doc, features = rows_ref.shape
    stack = Stack(sources, w_ref, sems, 4, heads * HEAD_DIM)

    @pl.when(step == 0)
    def _():
        stack.start()
        tables = table_copies(sources, tables_ref, sems, 4)
        for copy in tables:
            copy.start()
        norm_into(normed_ref, rows_ref, gain_ref)
        out_ref[...] = rows_ref[...].astype(F32)
        for copy in tables:
            copy.wait()
        table_into(table_ref, tables_ref, heads, buckets)
        stack.wait(0, 1, 2, 3)

    def weights(kind):
        start = pl.multiple_of(kind * features + step * HEAD_BLOCK, HEAD_BLOCK)
        return w_ref[pl.ds(start, HEAD_BLOCK)]

    for kind, ref in enumerate((q_ref, k_ref, v_ref)):
        ref[...] = dot_nt(normed_ref[...], weights(kind)).astype(BF16)
    none = jnp.zeros((doc, LANES), BF16)
    for pair in range(BLOCK_HEADS // 2):
        lanes = slice(pair * LANES, (pair + 1) * LANES)
        k, v_t = k_ref[:, lanes], flip(v_ref[:, lanes])
        q_t = flip(q_ref[:, lanes].astype(F32) * SCALE)
        k_of = [pick(which, k, none) for which in range(2)]
        for span in spans(doc, Q_BLOCK):
            rows, mixed = span.stop, []
            for which in range(2):
                h = 2 * pair + which
                bias = bias_block(table_ref, ids_ref, step * BLOCK_HEADS + h, rows, span.start)
                bias_ref[h, :rows, span] = bias.astype(BF16)
                s = dot_nn(k_of[which][:rows], q_t[:, span]) + bias
                top = jnp.max(s, axis=0, keepdims=True)
                p = jnp.exp(s - top)
                total = jnp.sum(p, axis=0, keepdims=True)
                mixed.append(dot_nn(v_t[half_rows(which), :rows], p.astype(BF16)) / total)
                lse_ref[0, h : h + 1, span] = top + jnp.log(total)
            mixed_ref[span, lanes] = jnp.concatenate(mixed, axis=0).T.astype(BF16)
    out_ref[...] += dot_nn(mixed_ref[...], weights(3))


def self_backward_kernel(heads, shares, *refs):
    count = shares // 2
    rows_ref, gain_ref, branch_ref, add_ref = refs[:4]
    q_ref, k_ref, v_ref, mixed_ref, lse_ref, bias_ref = refs[4:10]
    sources, refs = refs[10 : 10 + shares], refs[10 + shares :]
    hop_in, hop_out, refs = refs[: count - 1], refs[count - 1 : 2 * count - 2], refs[2 * count - 2 :]
    sums, refs = refs[:count], refs[count:]
    ds_ref, out_ref, gain_grad_ref = refs[:3]
    w_ref, normed_ref, g_ref, grad_ref, back_ref, give_ref, keep_ref, came_ref = refs[3:11]
    sems, swap_sems, hop_sems = refs[11:]
    step = pl.program_id(0)
    doc, features = rows_ref.shape
    half = features // 2
    stack = Stack(sources, w_ref, sems, 4, heads * HEAD_DIM)
    swap = to_differing(1, give_ref, came_ref, swap_sems)
    hops = [
        to_differing(2, source, target, hop_sems) for source, target in zip(hop_in, hop_out)
    ]

    @pl.when(step == 0)
    def _():
        stack.start()
        greet([1, 2][:count])
        for hop in hops:
            hop.start()
        norm_into(normed_ref, rows_ref, gain_ref)
        stack.wait(3)

    start = pl.multiple_of(3 * features + step * HEAD_BLOCK, HEAD_BLOCK)
    g_ref[...] = dot_nt(branch_ref[...], w_ref[pl.ds(start, HEAD_BLOCK)]).astype(BF16)
    none = jnp.zeros((doc, LANES), BF16)
    ones = extra_lanes(doc, None)
    for pair in range(BLOCK_HEADS // 2):
        lanes = lane_block(step * HEAD_BLOCK + pair * LANES)
        q, k, v = q_ref[:, lanes], k_ref[:, lanes], v_ref[:, lanes]
        g = g_ref[:, pair * LANES : (pair + 1) * LANES]
        q_t, k_t = q.astype(F32).T * SCALE, flip(k)
        g_t = g.astype(F32).T
        inner = g_t * mixed_ref[:, lanes].astype(F32).T
        per_head = []
        for which in range(2):
            h = 2 * pair + which
            minus = jnp.sum(inner[half_rows(which)], axis=0, keepdims=True)
            per_head.append(
                (
                    pick(which, k, ones),
                    pick(which, v, ones),
                    with_extra(which, q_t, False, lse_ref[0, h : h + 1, :]),
                    with_extra(which, g_t, False, minus),
                    pick(which, q, none),
                    pick(which, g, none),
                )
            )
        grad_k = grad_v = None
        for span in spans(doc, Q_BLOCK):
            rows, grad_q, part_k, part_v = span.stop, [], None, None
            for which, (k_of, v_of, q_with, g_with, q_of, g_of) in enumerate(per_head):
                h = 2 * pair + which
                s = dot_nn(k_of[:rows], q_with[:, span])
                p = jnp.exp(s + bias_ref[h, :rows, span].astype(F32))
                ds = (p * dot_nn(v_of[:rows], g_with[:, span])).astype(BF16)
                ds_ref[h, :rows, span] = ds
                grad_q.append(dot_nn(k_t[half_rows(which), :rows], ds))
                to_v = dot_nn(p.astype(BF16), g_of[span])
                to_k = dot_nn(ds, q_of[span])
                part_v = to_v if part_v is None else part_v + to_v
                part_k = to_k if part_k is None else part_k + to_k
            grad_q = (jnp.concatenate(grad_q, axis=0) * SCALE).T
            grad_ref[span, lanes] = grad_q.astype(BF16)
            if grad_v is not None:
                part_v = jnp.concatenate(
                    [part_v[: span.start] + grad_v, part_v[span.start :]], axis=0
                )
                part_k = jnp.concatenate(
                    [part_k[: span.start] + grad_k, part_k[span.start :]], axis=0
                )
            grad_v, grad_k = part_v, part_k
        k_lanes = lane_block(features + step * HEAD_BLOCK + pair * LANES)
        v_lanes = lane_block(2 * features + step * HEAD_BLOCK + pair * LANES)
        grad_ref[:, k_lanes] = (grad_k * SCALE).astype(BF16)
        grad_ref[:, v_lanes] = grad_v.astype(BF16)

    @pl.when(step == pl.num_programs(0) - 1)
    def _():
        stack.wait(0, 1, 2)
        def weight_grads(ref, columns):
            for kind in range(3):
                kind_columns = slice(kind * features + columns.start, kind * features + columns.stop)
                ref[kind] = dot_tn(grad_ref[:, kind_columns], normed_ref[...]).astype(BF16)
            ref[3] = dot_tn(mixed_ref[:, columns], branch_ref[...]).astype(BF16)

        weight_grads(give_ref, slice(0, half))
        swap.start()
        weight_grads(keep_ref, slice(half, features))
        gain_grad_ref[...] = jnp.zeros_like(gain_grad_ref)
        back_ref[...] = dot_nn(grad_ref[...], w_ref[: 3 * features])
        for span in spans(doc, ROW_BLOCK):
            norm_back_into(
                span, back_ref[span], out_ref, None, gain_grad_ref, rows_ref, gain_ref, add_ref
            )
        swap.wait_recv()
        rows = half // count
        for share, sums_ref in enumerate(sums):
            for kind in range(4):
                span = slice(share * rows, (share + 1) * rows)
                to = slice(kind * rows, (kind + 1) * rows)
                sums_ref[to] = low_sum(keep_ref[kind, span], came_ref[kind, span])
        swap.wait_send()
        for hop in hops:
            hop.wait()


def cross_forward_kernel(heads, shares, length_ref, rows_ref, gain_ref, memory_ref, *refs):
    sources = refs[:shares]
    q_ref, k_ref, v_ref, mixed_ref, lse_ref, out_ref = refs[shares : shares + 6]
    w_ref, normed_ref, extra_ref, p_ref, mix_ref, sems = refs[shares + 6 :]
    step = pl.program_id(0)
    (doc, features), slots = rows_ref.shape, memory_ref.shape[0]
    stack = Stack(sources, w_ref, sems, 4, heads * HEAD_DIM)

    @pl.when(step == 0)
    def _():
        stack.start()
        norm_into(normed_ref, rows_ref, gain_ref)
        out_ref[...] = rows_ref[...]
        slot = lax.broadcasted_iota(jnp.int32, (slots, LANES), 0)
        extra_ref[...] = extra_lanes(slots, slot < length_ref[0])
        stack.wait(0, 1, 2, 3)

    def weights(kind):
        start = pl.multiple_of(kind * features + step * HEAD_BLOCK, HEAD_BLOCK)
        return w_ref[pl.ds(start, HEAD_BLOCK)]

    q_ref[...] = dot_nt(normed_ref[...], weights(0)).astype(BF16)
    k_ref[...] = dot_nt(memory_ref[...], weights(1)).astype(BF16)
    v_ref[...] = dot_nt(memory_ref[...], weights(2)).astype(BF16)

    units = [
        (pair, which, span)
        for pair in range(BLOCK_HEADS // 2)
        for span in spans(doc, Q_BLOCK)
        for which in range(2)
    ]
    ones = jnp.ones((TILE_ROWS, slots), BF16)
    keys = spans(slots, FORWARD_K_BLOCK)

    def lanes_of(pair):
        return slice(pair * LANES, (pair + 1) * LANES)

    def key_side(pair, which):
        return pick(which, k_ref[:, lanes_of(pair)], extra_ref[...])

    def write(pair, which, span, top, total, mixed):
        h = 2 * pair + which
        lse_ref[0, h : h + 1, span] = top + jnp.log(total)
        mix_ref[half_rows(which)] = mixed / total
        if which == 1:
            mixed_ref[span, lanes_of(pair)] = mix_ref[...].T.astype(BF16)

    v_t = [flip(v_ref[:, lanes_of(p)]) for p in range(BLOCK_HEADS // 2)]
    q_t = [q_ref[:, lanes_of(p)].astype(F32).T * SCALE for p in range(BLOCK_HEADS // 2)]

    def begin(unit):
        pair, which, span = unit
        k_of = key_side(pair, which)
        s = dot_nn(k_of[keys[0]], with_extra(which, q_t[pair][:, span], True, None))
        top = jnp.max(s, axis=0, keepdims=True)
        return k_of, s, top, with_extra(which, q_t[pair][:, span], True, top)

    worst = jnp.zeros((1, Q_BLOCK), F32)
    ahead = begin(units[0])
    for i, (pair, which, span) in enumerate(units):
        (k_of, s, top, q_with), slot = ahead, i % 2
        p_ref[slot, keys[0]] = jnp.exp(s - top).astype(BF16)
        for rows in keys[1:]:
            p_ref[slot, rows] = jnp.exp(dot_nn(k_of[rows], q_with)).astype(BF16)
        if i + 1 < len(units):
            ahead = begin(units[i + 1])
        value_side = jnp.concatenate([v_t[pair][half_rows(which)], ones], axis=0)
        mixed = dot_nn(value_side, p_ref[slot])
        total = mixed[HEAD_DIM : HEAD_DIM + 1]
        worst = jnp.maximum(worst, total)
        write(pair, which, span, top, total, mixed[:HEAD_DIM])

    @pl.when(jnp.max(worst) > LARGEST_SUM)
    def _():
        for pair, which, span in units:
            q_with = with_extra(
                which, q_ref[:, lanes_of(pair)].astype(F32).T[:, span] * SCALE, True, None
            )
            k_of = key_side(pair, which)
            s = [dot_nn(k_of[rows], q_with) for rows in keys]
            top = functools.reduce(jnp.maximum, [jnp.max(c, axis=0, keepdims=True) for c in s])
            total = jnp.zeros_like(top)
            for rows, chunk in zip(keys, s):
                p = jnp.exp(chunk - top)
                total = total + jnp.sum(p, axis=0, keepdims=True)
                p_ref[0, rows] = p.astype(BF16)
            mixed = dot_nn(flip(v_ref[:, lanes_of(pair)])[half_rows(which)], p_ref[0])
            write(pair, which, span, top, total, mixed)

    out_ref[...] += dot_nn(mixed_ref[...], weights(3))


def cross_backward_kernel(heads, shares, size, scattered, hops_wanted, length_ref, *refs):
    gain_ref, branch_ref, q_ref, mixed_ref, lse_ref = refs[:5]
    rows_in, memory_in, add_in, k_in, v_in = refs[5:10]
    sources = refs[10 : 10 + shares]
    count = shares // 2
    refs = refs[10 + shares :]
    scatter_in, refs = refs[:scattered], refs[scattered:]
    hidden_in, refs = refs[:hops_wanted], refs[hops_wanted:]
    hidden_out, refs = refs[:hops_wanted], refs[hops_wanted:]
    if scattered:
        scatter_out, refs = refs[0], refs[1:]
        (part_ref, ring_slots, done_ref, scatter_came), refs = refs[-8:-4], refs[:-8] + refs[-4:]
        (ring_send, ring_came, part_sems, done_sems), refs = refs[-4:], refs[:-4]
        scatter = Scatter(size, part_ref, ring_slots, done_ref, ring_send, ring_came)
        part_loads = [
            pltpu.make_async_copy(source, part_ref.at[i], part_sems.at[i])
            for i, source in enumerate(scatter_in)
        ]
        for copy in part_loads:
            copy.start()
    sums, refs = refs[:count], refs[count:]
    memory_out, out_ref, low_ref, gain_grad_ref = refs[:4]
    rows_ref, memory_ref, add_ref, k_ref, v_ref = refs[4:9]
    (
        w_ref,
        normed_ref,
        extra_ref,
        g_ref,
        grad_q_ref,
        grad_ref,
        ds_ref,
        give_ref,
        keep_ref,
        came_ref,
        memory_grad_ref,
        back_ref,
        sems,
        load_sems,
        key_sems,
        out_sems,
        swap_sems,
        hop_sems,
    ) = refs[9:]
    (doc, features), slots = rows_ref.shape, memory_ref.shape[0]
    half, blocks = features // 2, features // HEAD_BLOCK
    stack = Stack(sources, w_ref, sems, 4, heads * HEAD_DIM)
    loads = [
        pltpu.make_async_copy(source, target, load_sems.at[i])
        for i, (source, target) in enumerate(
            ((memory_in, memory_ref), (rows_in, rows_ref), (add_in, add_ref))
        )
    ]

    def key_copies(b):
        lanes = pl.ds(pl.multiple_of(b * HEAD_BLOCK, HEAD_BLOCK), HEAD_BLOCK)
        return [
            pltpu.make_async_copy(source.at[:, lanes], target.at[b], key_sems.at[i, b])
            for i, (source, target) in enumerate(((k_in, k_ref), (v_in, v_ref)))
        ]

    stack.start()
    for b in range(blocks):
        for copy in key_copies(b):
            copy.start()
    for copy in loads:
        copy.start()
    greet([1, 2][:count], [way[1] for way in ring_ways(size)] if scattered else [])
    hops = [
        to_differing(2, source, target, hop_sems.at[i])
        for i, (source, target) in enumerate(zip(hidden_in, hidden_out))
    ]
    for hop in hops:
        hop.start()
    if scattered:
        for copy in part_loads:
            copy.wait()
        scatter.begin()
    slot = lax.broadcasted_iota(jnp.int32, (slots, LANES), 0)
    extra_ref[...] = extra_lanes(slots, slot < length_ref[0])
    none = jnp.zeros((doc, LANES), BF16)
    stack.wait(3)

    def one_block(step, carry):
        start = pl.multiple_of(3 * features + step * HEAD_BLOCK, HEAD_BLOCK)
        g_ref[...] = dot_nt(branch_ref[...], w_ref[pl.ds(start, HEAD_BLOCK)]).astype(BF16)
        for copy in key_copies(step):
            copy.wait()
        for pair in range(BLOCK_HEADS // 2):
            local = slice(pair * LANES, (pair + 1) * LANES)
            lanes = lane_block(step * HEAD_BLOCK + pair * LANES)
            v_lanes = lane_block(features + step * HEAD_BLOCK + pair * LANES)
            q, g = q_ref[:, lanes], g_ref[:, local]
            q_t, g_t = q.astype(F32).T * SCALE, g.astype(F32).T
            inner = g_t * mixed_ref[:, lanes].astype(F32).T
            per_head = []
            for which in range(2):
                h = 2 * pair + which
                minus = jnp.sum(inner[half_rows(which)], axis=0, keepdims=True)
                per_head.append(
                    (
                        with_extra(which, q_t, True, lse_ref[step, h : h + 1, :]),
                        with_extra(which, g_t, False, minus),
                        pick(which, q, none),
                        pick(which, g, none),
                    )
                )
            for rows in spans(slots, K_BLOCK):
                k, v, extra = k_ref[step, rows, local], v_ref[step, rows, local], extra_ref[rows]
                part_k = part_v = None
                for which, (q_with, g_with, q_of, g_of) in enumerate(per_head):
                    p = jnp.exp(dot_nn(pick(which, k, extra), q_with))
                    ds = (p * dot_nn(pick(which, v, extra), g_with)).astype(BF16)
                    ds_ref[which, rows] = ds
                    to_v = dot_nn(p.astype(BF16), g_of)
                    to_k = dot_nn(ds, q_of)
                    part_v = to_v if part_v is None else part_v + to_v
                    part_k = to_k if part_k is None else part_k + to_k
                grad_ref[rows, lanes] = (part_k * SCALE).astype(BF16)
                grad_ref[rows, v_lanes] = part_v.astype(BF16)
            k_t = flip(k_ref[step, :, local])
            grad_q = [dot_nn(k_t[half_rows(which)], ds_ref[which]) for which in range(2)]
            grad_q_ref[:, lanes] = (jnp.concatenate(grad_q, axis=0) * SCALE).T.astype(BF16)
            if scattered:
                scatter_step(1 + step * (BLOCK_HEADS // 2) + pair)
        return carry

    places = blocks * (BLOCK_HEADS // 2)

    def scatter_step(step):
        if size - 2 >= places:
            scatter.advance(step)
        elif size > 2:

            @pl.when(step <= size - 2)
            def _():
                scatter.advance(step)

    lax.fori_loop(0, blocks, one_block, 0)
    if scattered:

        def rest(step, carry):
            scatter.advance(step)
            return carry

        lax.fori_loop(min(places, size - 2) + 1, size - 1, rest, 0)
        scatter.turn()
        done_hops = [
            to_differing(2, done_ref.at[:, i], scatter_came, done_sems)
            for i in range(1, scattered)
        ]
        for hop in done_hops:
            hop.start()

    for copy in loads:
        copy.wait()
    norm_into(normed_ref, rows_ref, gain_ref)

    def weight_grads(ref, first):
        columns = slice(first, first + half)
        v_columns = slice(features + first, features + first + half)
        ref[0] = dot_tn(grad_q_ref[:, columns], normed_ref[...]).astype(BF16)
        ref[1] = dot_tn(grad_ref[:, columns], memory_ref[...]).astype(BF16)
        ref[2] = dot_tn(grad_ref[:, v_columns], memory_ref[...]).astype(BF16)
        ref[3] = dot_tn(mixed_ref[:, columns], branch_ref[...]).astype(BF16)

    weight_grads(give_ref, 0)
    swap = to_differing(1, give_ref, came_ref, swap_sems)
    swap.start()
    stack.wait(0, 1, 2)
    writes = []
    for i, rows in enumerate(spans(slots, MEMORY_BLOCK)):
        memory_grad_ref[rows] = dot_nn(
            grad_ref[rows], w_ref[features : 3 * features]
        ).astype(BF16)
        writes.append(
            pltpu.make_async_copy(memory_grad_ref.at[rows], memory_out.at[rows], out_sems.at[i])
        )
        writes[-1].start()
    weight_grads(keep_ref, half)
    gain_grad_ref[...] = jnp.zeros_like(gain_grad_ref)
    back_ref[...] = dot_nn(grad_q_ref[...], w_ref[:features])
    for span in spans(doc, ROW_BLOCK):
        norm_back_into(
            span, back_ref[span], out_ref, low_ref, gain_grad_ref, rows_ref, gain_ref, add_ref
        )
    swap.wait_recv()
    rows = half // count
    for share, sums_ref in enumerate(sums):
        for kind in range(4):
            span = slice(share * rows, (share + 1) * rows)
            to = slice(kind * rows, (kind + 1) * rows)
            sums_ref[to] = low_sum(keep_ref[kind, span], came_ref[kind, span])
    swap.wait_send()
    for copy in writes:
        copy.wait()
    for hop in hops:
        hop.wait()
    if scattered:
        for hop in done_hops:
            hop.wait()
        own = done_ref[:, 0]
        scatter_out[...] = low_sum(own, scatter_came[...]) if done_hops else own
        scatter.wait_sent()


def feed_forward_kernel(first, last, rows_ref, gain_ref, cotangent_ref, *refs):
    sources, refs = refs[:2], refs[2:]
    if not first:
        before_in, refs = refs[:2], refs[2:]
    sums, layer_ref, out_ref = refs[:2], refs[2], refs[3]
    if last:
        low_ref, gain_grad_ref = refs[4:6]
        refs = refs[2:]
    (
        wide_ref,
        narrow_ref,
        normed_ref,
        normed_t,
        cotangent_t,
        active_ref,
        grad_ref,
        give_ref,
        keep_ref,
        came_ref,
        layer_in_ref,
        back_in_ref,
        product_ref,
        sems,
        before_sems,
        swap_sems,
    ) = refs[4:]
    step, steps = pl.program_id(0), pl.num_programs(0)
    half = steps // 2
    doc = rows_ref.shape[0]
    hidden = sources[0].shape[0] // 2
    copies = [
        [
            pltpu.make_async_copy(
                source.at[pl.ds(kind * hidden, hidden)],
                stack.at[pl.ds(p * hidden, hidden)],
                sems.at[p, kind],
            )
            for kind, stack in enumerate((wide_ref, narrow_ref))
        ]
        for p, source in enumerate(sources)
    ]
    loads = []
    if not first:
        loads = [
            pltpu.make_async_copy(source, target, before_sems.at[i])
            for i, (source, target) in enumerate(zip(before_in, (layer_in_ref, back_in_ref)))
        ]
    swap = to_differing(1, give_ref, came_ref, swap_sems)

    @pl.when(step == 0)
    def _():
        for pair in copies:
            for copy in pair:
                copy.start()
        for copy in loads:
            copy.start()
        greet([1])
        norm_into(normed_ref, rows_ref, gain_ref)
        for span in spans(doc, ROW_BLOCK):
            normed_t[:, span] = flip(normed_ref[span])
            cotangent_t[:, span] = flip(cotangent_ref[span])

    for p, pair in enumerate(copies):

        @pl.when(step == p * half)
        def _(pair=pair):
            for copy in pair:
                copy.wait()

    units = pl.ds(pl.multiple_of(step * HIDDEN_BLOCK, HIDDEN_BLOCK), HIDDEN_BLOCK)
    activated, slope = gelu_and_slope(dot_nn(wide_ref[units], normed_t[...]))
    active_ref[units] = activated.astype(BF16)
    grad_ref[units] = (dot_nn(narrow_ref[units], cotangent_t[...]) * slope).astype(BF16)

    def store(ref, at):
        rows = pl.ds(pl.multiple_of(at * HIDDEN_BLOCK, HIDDEN_BLOCK), HIDDEN_BLOCK)
        ref[0, rows] = dot_nn(grad_ref[units], normed_ref[...]).astype(BF16)
        ref[1, rows] = dot_nn(active_ref[units], cotangent_ref[...]).astype(BF16)

    @pl.when(step < half)
    def _():
        store(give_ref, step)

    @pl.when(step == half - 1)
    def _():
        swap.start()

    @pl.when(step >= half)
    def _():
        store(keep_ref, step - half)

    @pl.when(step == steps - 1)
    def _():
        for copy in loads:
            copy.wait()
        if last:
            gain_grad_ref[...] = jnp.zeros_like(gain_grad_ref)
        product_ref[...] = dot_tn(active_ref[...], narrow_ref[...])
        for span in spans(doc, ROW_BLOCK):
            layer = rows_ref[span] if first else layer_in_ref[span]
            layer_ref[span] = (layer + product_ref[span]).astype(layer_ref.dtype)
        product_ref[...] = dot_tn(grad_ref[...], wide_ref[...])
        for span in spans(doc, ROW_BLOCK):
            back = product_ref[span]
            if not first:
                back = back + back_in_ref[span]
            if last:
                norm_back_into(
                    span, back, out_ref, low_ref, gain_grad_ref, rows_ref, gain_ref, cotangent_ref
                )
            else:
                out_ref[span] = back
        swap.wait_recv()
        for kind, sums_ref in enumerate(sums):
            for span in spans(hidden, HIDDEN_BLOCK):
                sums_ref[span] = low_sum(keep_ref[kind, span], came_ref[kind, span])
        swap.wait_send()


def pack_kernel(flipped, *refs):
    out_ref, start = refs[-1], 0
    for source, turn in zip(refs[:-1], flipped):
        if source.shape[-1] != out_ref.shape[1] and not turn:
            out_ref[start:] = jnp.zeros((TABLE_ROWS, out_ref.shape[1]), BF16)
            out_ref[start : start + source.shape[0], : source.shape[1]] = source[...]
            continue
        rows = source.shape[1] if turn else source.shape[0]
        span = slice(start, start + rows)
        out_ref[span] = flip(source[...]) if turn else source[...]
        start += rows


def finish_kernel(*refs):
    sources, outs, refs = refs[:4], refs[4:14], refs[14:]
    ins, wides, in_sems, out_sems = refs[:4], refs[4:14], refs[14], refs[15]
    loads, writes = [], []
    for i, (source, target) in enumerate(zip(sources, ins)):
        for j, span in enumerate(spans(target.shape[0], FINISH_BLOCK)):
            loads.append(
                pltpu.make_async_copy(source.at[span], target.at[span], in_sems.at[i, j])
            )
            loads[-1].start()

    def write(i, part):
        writes.append(
            pltpu.make_async_copy(wides[i].at[part], outs[i].at[part], out_sems.at[len(writes)])
        )
        writes[-1].start()

    waiting = iter(loads)
    hidden = wides[1].shape[0]
    for span in spans(hidden, FINISH_BLOCK):
        next(waiting).wait()
        for part in spans(FINISH_BLOCK, LANES):
            rows = slice(span.start + part.start, span.start + part.stop)
            wides[0][:, rows] = ins[0][rows].astype(F32).T
        write(0, (slice(None), span))
    for span in spans(hidden, FINISH_BLOCK):
        next(waiting).wait()
        wides[1][span] = ins[1][span].astype(F32)
        write(1, span)
    for i in (2, 3):
        for _ in spans(ins[i].shape[0], FINISH_BLOCK):
            next(waiting).wait()
        rows = wides[2].shape[0]
        for kind in range(4):
            at = 2 + 4 * (i - 2) + kind
            wides[at][...] = ins[i][kind * rows : (kind + 1) * rows].astype(F32)
            write(at, slice(None))
    for copy in writes:
        copy.wait()


def params():
    return pltpu.CompilerParams(vmem_limit_bytes=VMEM_BYTES)


def cost(flops=1 << 20):
    return pl.CostEstimate(flops=flops, bytes_accessed=1 << 16, transcendentals=0)


def shape(dims, dtype):
    return jax.ShapeDtypeStruct(dims, dtype)


def whole(array):
    return pl.BlockSpec(
        array.shape, lambda *_: (0,) * len(array.shape), pipeline_mode=pl.Buffered(1)
    )


def result(array):
    return pl.BlockSpec(array.shape, lambda *_: (0,) * len(array.shape))


def columns(rows):
    return pl.BlockSpec((rows, HEAD_BLOCK), lambda i: (0, i))


def anywhere(arrays):
    return [pl.BlockSpec(memory_space=pl.ANY) for _ in arrays]


SCALAR = pl.BlockSpec(memory_space=pltpu.SMEM)


def call(
    kernel, name, grid, in_specs, out_specs, out_shape, scratch, args, channel=None, flops=1 << 20
):
    compiler_params = params()
    if channel is not None:
        compiler_params = pltpu.CompilerParams(
            vmem_limit_bytes=VMEM_BYTES, collective_id=channel, has_side_effects=True
        )
    return pl.pallas_call(
        kernel,
        grid=grid,
        in_specs=in_specs,
        out_specs=out_specs,
        out_shape=out_shape,
        scratch_shapes=scratch,
        compiler_params=compiler_params,
        cost_estimate=cost(flops),
        name=name,
    )(*args)


def pack(*parts):
    arrays, flipped = zip(*parts)
    features = arrays[0].shape[0] if flipped[0] else arrays[0].shape[1]
    rows = [a.shape[1] if turn else a.shape[0] for a, turn in parts]
    if arrays[-1].shape[1] < features and not flipped[-1]:
        rows[-1] = TABLE_ROWS
    rows = sum(rows)
    return pl.pallas_call(
        functools.partial(pack_kernel, flipped),
        out_shape=shape((rows, features), BF16),
        compiler_params=params(),
        cost_estimate=cost(),
        name="pack",
    )(*arrays)


def self_forward(heads, buckets, rows, gain, weights, ids):
    doc, features = rows.shape
    shares, steps = len(weights), features // HEAD_BLOCK
    narrow, tall = shape((doc, features), BF16), shape((doc, features), F32)
    scores = shape((steps * BLOCK_HEADS, doc, doc), BF16)
    out_shape = (*[narrow] * 4, shape((steps, 8, doc), F32), scores, tall)
    return call(
        functools.partial(self_forward_kernel, heads, buckets, shares),
        "self_forward",
        (steps,),
        [whole(rows), whole(gain), whole(ids), *anywhere(weights)],
        (
            *[columns(doc)] * 4,
            pl.BlockSpec((1, 8, doc), lambda i: (i, 0, 0)),
            pl.BlockSpec((BLOCK_HEADS, doc, doc), lambda i: (i, 0, 0)),
            result(tall),
        ),
        out_shape,
        [
            pltpu.VMEM((4 * features, features), BF16),
            pltpu.VMEM((shares, TABLE_ROWS, features), BF16),
            pltpu.VMEM((TABLE_ROWS, LANES), F32),
            pltpu.VMEM((doc, features), BF16),
            pltpu.SemaphoreType.DMA((shares, 5)),
        ],
        (rows, gain, ids, *weights),
    )


def self_backward(heads, rows, gain, branch, add, saved, weights, hops):
    doc, features = rows.shape
    shares, steps = len(weights), features // HEAD_BLOCK
    count = shares // 2
    *arrays, lse, bias = saved
    packed = pltpu.VMEM((4, features // 2, features), BF16)
    scores = pl.BlockSpec((BLOCK_HEADS, doc, doc), lambda i: (i, 0, 0))
    out_shape = (
        *[shape(h.shape, BF16) for h in hops],
        *[shape((4 * heads * HEAD_DIM, features), BF16)] * count,
        shape((steps * BLOCK_HEADS, doc, doc), BF16),
        shape((doc, features), F32),
        shape((8, features), F32),
    )
    return call(
        functools.partial(self_backward_kernel, heads, shares),
        "self_backward",
        (steps,),
        [
            *[whole(a) for a in (rows, gain, branch, add, *arrays)],
            pl.BlockSpec((1, 8, doc), lambda i: (i, 0, 0)),
            scores,
            *anywhere(weights),
            *anywhere(hops),
        ],
        (
            *anywhere(hops),
            *[result(o) for o in out_shape[len(hops) : len(hops) + count]],
            scores,
            result(out_shape[-2]),
            result(out_shape[-1]),
        ),
        out_shape,
        [
            pltpu.VMEM((4 * features, features), BF16),
            pltpu.VMEM((doc, features), BF16),
            pltpu.VMEM((doc, HEAD_BLOCK), BF16),
            pltpu.VMEM((doc, 3 * features), BF16),
            pltpu.VMEM((doc, features), F32),
            packed,
            packed,
            packed,
            pltpu.SemaphoreType.DMA((shares, 4)),
            pltpu.SemaphoreType.DMA((2,)),
            pltpu.SemaphoreType.DMA((2,)),
        ],
        (rows, gain, branch, add, *arrays, lse, bias, *weights, *hops),
        channel=4,
    )


def cross_forward(heads, rows, gain, memory, length, weights):
    (doc, features), slots = rows.shape, memory.shape[0]
    shares, steps = len(weights), features // HEAD_BLOCK
    query, key = shape((doc, features), BF16), shape((slots, features), BF16)
    tall = shape((doc, features), F32)
    return call(
        functools.partial(cross_forward_kernel, heads, shares),
        "cross_forward",
        (steps,),
        [SCALAR, whole(rows), whole(gain), whole(memory), *anywhere(weights)],
        (
            columns(doc),
            columns(slots),
            columns(slots),
            columns(doc),
            pl.BlockSpec((1, 8, doc), lambda i: (i, 0, 0)),
            result(tall),
        ),
        (query, key, key, query, shape((steps, 8, doc), F32), tall),
        [
            pltpu.VMEM((4 * features, features), BF16),
            pltpu.VMEM((doc, features), BF16),
            pltpu.VMEM((slots, LANES), BF16),
            pltpu.VMEM((2, slots, Q_BLOCK), BF16),
            pltpu.VMEM((LANES, Q_BLOCK), F32),
            pltpu.SemaphoreType.DMA((shares, 4)),
        ],
        (length, rows, gain, memory, *weights),
    )


def cross_backward(
    heads, size, rows, gain, memory, length, branch, add, saved, weights, scattered, hops
):
    (doc, features), slots = rows.shape, memory.shape[0]
    shares, blocks = len(weights), features // HEAD_BLOCK
    count = shares // 2
    blocks_out, ring_scratch = [], []
    if scattered:
        number, part = len(scattered), scattered[0].shape
        block = (2, part[0] // (2 * size), features)
        blocks_out = [shape(block, BF16)]
        steps = pltpu.SemaphoreType.DMA((2, size - 1))
        ring_scratch = [
            pltpu.VMEM((number, *part), BF16),
            pltpu.VMEM((2, size - 1, number, *block[1:]), BF16),
            pltpu.VMEM((2, number, *block[1:]), BF16),
            pltpu.VMEM(block, BF16),
            steps,
            steps,
            pltpu.SemaphoreType.DMA((number,)),
            pltpu.SemaphoreType.DMA((2,)),
        ]
    out_shape = (
        *[shape(h.shape, BF16) for h in hops],
        *blocks_out,
        *[shape((4 * heads * HEAD_DIM, features), BF16)] * count,
        shape((slots, features), BF16),
        shape((doc, features), F32),
        shape((doc, features), BF16),
        shape((8, features), F32),
    )
    query, key, value, mixed, lse = saved
    near = (gain, branch, query, mixed, lse)
    far = (rows, memory, add, key, value, *weights, *scattered, *hops)
    vmem, hbm = pl.BlockSpec(memory_space=pltpu.VMEM), pl.BlockSpec(memory_space=pl.ANY)
    packed = pltpu.VMEM((4, features // 2, features), BF16)
    key_block = pltpu.VMEM((blocks, slots, HEAD_BLOCK), BF16)
    return call(
        functools.partial(
            cross_backward_kernel, heads, shares, size, len(scattered), len(hops)
        ),
        "cross_backward",
        (),
        [SCALAR, *[vmem for _ in near], *[hbm for _ in far]],
        (
            *[hbm] * len(hops),
            *[vmem] * len(blocks_out),
            *[vmem] * count,
            hbm,
            vmem,
            vmem,
            vmem,
        ),
        out_shape,
        [
            pltpu.VMEM((doc, features), F32),
            pltpu.VMEM((slots, features), BF16),
            pltpu.VMEM((doc, features), F32),
            key_block,
            key_block,
            pltpu.VMEM((4 * features, features), BF16),
            pltpu.VMEM((doc, features), BF16),
            pltpu.VMEM((slots, LANES), BF16),
            pltpu.VMEM((doc, HEAD_BLOCK), BF16),
            pltpu.VMEM((doc, features), BF16),
            pltpu.VMEM((slots, 2 * features), BF16),
            pltpu.VMEM((2, slots, doc), BF16),
            packed,
            packed,
            packed,
            pltpu.VMEM((slots, features), BF16),
            pltpu.VMEM((doc, features), F32),
            pltpu.SemaphoreType.DMA((shares, 4)),
            pltpu.SemaphoreType.DMA((3,)),
            pltpu.SemaphoreType.DMA((2, blocks)),
            pltpu.SemaphoreType.DMA((slots // MEMORY_BLOCK,)),
            pltpu.SemaphoreType.DMA((2,)),
            pltpu.SemaphoreType.DMA((max(len(hops), 1), 2)),
            *ring_scratch,
        ],
        (length, *near, *far),
        channel=1,
    )


def feed_forward(rows, gain, cotangent, weights, before, last):
    (doc, features), shares = rows.shape, len(weights)
    share = weights[0].shape[0] // 2
    hidden = share * shares
    steps = hidden // HIDDEN_BLOCK
    summed, tall = shape((share, features), BF16), shape((doc, features), F32)
    low = shape((doc, features), BF16)
    rest = [low, tall, low, shape((8, features), F32)] if last else [tall, tall]
    kept, added = pltpu.VMEM((2, share, features), BF16), pltpu.VMEM(tall.shape, F32)
    return call(
        functools.partial(feed_forward_kernel, not before, last),
        "feed_forward",
        (steps,),
        [whole(rows), whole(gain), whole(cotangent), *anywhere(weights), *anywhere(before)],
        (result(summed), result(summed), *[result(o) for o in rest]),
        (summed, summed, *rest),
        [
            pltpu.VMEM((hidden, features), BF16),
            pltpu.VMEM((hidden, features), BF16),
            pltpu.VMEM((doc, features), BF16),
            pltpu.VMEM((features, doc), BF16),
            pltpu.VMEM((features, doc), BF16),
            pltpu.VMEM((hidden, doc), BF16),
            pltpu.VMEM((hidden, doc), BF16),
            kept,
            kept,
            kept,
            added,
            added,
            added,
            pltpu.SemaphoreType.DMA((shares, 2)),
            pltpu.SemaphoreType.DMA((2,)),
            pltpu.SemaphoreType.DMA((2,)),
        ],
        (rows, gain, cotangent, *weights, *before),
        channel=3 if before else 2,
    )


def finish(sum_wide, sum_narrow, sum_cross, sum_self):
    rows, features = sum_self.shape
    hidden, part = sum_wide.shape[0], shape((rows // 4, features), F32)
    out_shape = [shape((features, hidden), F32), shape((hidden, features), F32), *[part] * 8]
    sources = (sum_wide, sum_narrow, sum_cross, sum_self)
    writes = 2 * hidden // FINISH_BLOCK + 8
    wide, narrow, *parts = pl.pallas_call(
        finish_kernel,
        in_specs=anywhere(sources),
        out_specs=anywhere(out_shape),
        out_shape=out_shape,
        scratch_shapes=[
            *[pltpu.VMEM(source.shape, BF16) for source in sources],
            *[pltpu.VMEM(out.shape, F32) for out in out_shape],
            pltpu.SemaphoreType.DMA((4, hidden // FINISH_BLOCK)),
            pltpu.SemaphoreType.DMA((writes,)),
        ],
        compiler_params=params(),
        cost_estimate=cost(),
        name="finish",
    )(*sources)
    return wide, narrow, parts[4:], parts[:4]


def share_place(row, other, peers):
    j, bit = 0, 1
    while bit < peers:
        j = j + bit * ((row // bit + other // bit) % 2)
        bit *= 2
    return (j % 2) * (j // 2) + (1 - j % 2) * (peers // 2 + j // 2)


def tail_kernel(size, peers, buckets, heads, gathered, counts, *refs):
    parts = []
    for count in counts:
        parts.append(refs[:count])
        refs = refs[count:]
    arrays, shares = len(counts) + 1, peers // 2
    last_refs, refs = refs[:shares], refs[shares:]
    ids_ref, ds_ref, *gain_refs = refs[:5]
    outs, small_out_ref, refs = refs[5 : 5 + arrays], refs[5 + arrays], refs[6 + arrays :]
    slots, refs = refs[:arrays], refs[arrays:]
    firsts, refs = refs[:arrays], refs[arrays:]
    far_came_ref, part_ref, scores_ref, bucket_ref = refs[:4]
    small_ref, near_ref, far_ref = refs[4:7]
    send, came, send_out, came_out, small_sems, hop_sems, local_sems = refs[7:]
    parts.append((part_ref,))
    me, row = lax.axis_index("dp"), lax.axis_index("mp")
    ways = ring_ways(size)
    doc = ids_ref.shape[0]
    mesh = pl.DeviceIdType.MESH

    load_scores = pltpu.make_async_copy(ds_ref, scores_ref, local_sems.at[0])
    load_scores.start()

    barrier = pltpu.get_barrier_semaphore()

    def greet(t, carry):
        pl.semaphore_signal(
            barrier, inc=1, device_id=((me + t) % size, row), device_id_type=mesh
        )
        return carry

    lax.fori_loop(1, size, greet, 0)
    for t in range(1, peers):
        pl.semaphore_signal(
            barrier, inc=1, device_id=(me, (row + t) % peers), device_id_type=mesh
        )
    pl.semaphore_wait(barrier, size - 1 + peers - 1)

    def block(i, way, number):
        rows = outs[i].shape[0] // (2 * size)
        return pl.ds(pl.multiple_of((way * size + number) * rows, 16), rows)

    def part(i, span):
        total = parts[i][0][span].astype(F32)
        for ref in parts[i][1:]:
            total = total + ref[span].astype(F32)
        return total

    def first_copy(i, way):
        return remote(
            firsts[i].at[way],
            slots[i].at[way, 0],
            send.at[i, way, 0],
            came.at[i, way, 0],
            (ways[way][1], row),
        )

    def next_copy(i, way, step):
        return remote(
            slots[i].at[way, step - 1],
            slots[i].at[way, step],
            send.at[i, way, step],
            came.at[i, way, step],
            (ways[way][1], row),
        )

    def wait_came(i, way, step):
        remote(
            slots[i].at[way, step],
            slots[i].at[way, step],
            send.at[i, way, step],
            came.at[i, way, step],
            (ways[way][1], row),
        ).wait_recv()

    def out_copy(i, way, step):
        span = block(i, way, (ways[way][0] + 1 - step + size) % size)
        return remote(
            outs[i].at[span],
            outs[i].at[span],
            send_out.at[i, way, step],
            came_out.at[i, way, step],
            (ways[way][1], row),
        )

    def begin(rings):
        for i, way in rings:
            firsts[i][way] = part(i, block(i, way, ways[way][0])).astype(BF16)
            first_copy(i, way).start()

    def plus_part(i, way, step):
        span = block(i, way, (ways[way][0] - step - 1 + size) % size)
        total = slots[i][way, step].astype(F32) + part(i, span)
        return span, total.astype(BF16)

    def advance(rings, step):
        for i, way in rings:
            wait_came(i, way, step - 1)
            slots[i][way, step - 1] = plus_part(i, way, step - 1)[1]
            next_copy(i, way, step).start()

    def turn(rings):
        for i, way in rings:
            wait_came(i, way, size - 2)
            span, total = plus_part(i, way, size - 2)
            outs[i][span] = total
            out_copy(i, way, 0).start()

    def pass_on(rings, step):
        for i, way in rings:
            out_copy(i, way, step - 1).wait_recv()
            out_copy(i, way, step).start()

    ready = [(i, way) for i in range(gathered) for way in range(2)]
    early = [(i, way) for i in range(gathered, arrays - 1) for way in range(2)]
    late = [(arrays - 1, way) for way in range(2)]

    other_chip = None
    if shares == 2:
        other_chip = to_differing(2, last_refs[1], far_came_ref, hop_sems)
        other_chip.start()
    begin(early)
    for i, way in ready:
        outs[i][block(i, way, (ways[way][0] + 1) % size)] = parts[i][0][way]
        out_copy(i, way, 0).start()

    rows_used, per_row = bucket_ref.shape[0], ds_ref.shape[0] // bucket_ref.shape[0]
    units = rows_used * buckets
    per_round = -(-units // max(2 * (size - 2), 1))

    def bucket_unit(u, carry):
        r, b = u // buckets, u % buckets
        sums = [jnp.zeros((8, LANES), F32) for _ in range(per_row)]
        for c in range(0, doc, LANES):
            hit = ids_ref[: c + LANES, c : c + LANES] == b
            for h in range(per_row):
                grads = scores_ref[r * per_row + h, : c + LANES, c : c + LANES].astype(F32)
                kept = jnp.where(hit, grads, 0.0).reshape(-1, 8, LANES)
                sums[h] = sums[h] + jnp.sum(kept, axis=0)
        for h in range(per_row):
            bucket_ref[r, h, pl.ds(b, 1), :] = jnp.sum(sums[h], axis=0, keepdims=True)
        return carry

    def bucket_round(k):
        low = jnp.minimum(k * per_round, units)
        lax.fori_loop(low, jnp.minimum(low + per_round, units), bucket_unit, 0)

    bucket_ref[...] = jnp.zeros_like(bucket_ref)
    part_ref[...] = jnp.zeros_like(part_ref)
    load_scores.wait()

    def early_step(step, carry):
        advance(early, step)
        pass_on(ready, step)
        bucket_round(step - 1)
        return carry

    begin_late = LATE_STEP if size - 1 > LATE_STEP else size - 1
    lax.fori_loop(1, min(begin_late + 1, size - 1), early_step, 0)
    if begin_late == size - 1:
        turn(early)
    used = slice(0, last_refs[0].shape[0])
    if other_chip is None:
        part_ref[used] = last_refs[0][...]
    else:
        other_chip.wait_recv()
        part_ref[used] = low_sum(last_refs[0][...], far_came_ref[...])
    begin(late)

    def both_step(step, carry):
        early_step(step, carry)
        advance(late, step - begin_late)
        return carry

    def middle_step(step, carry):
        pass_on(early, step)
        advance(late, step + size - 1 - begin_late)
        bucket_round(size - 2 + step - 1)
        return carry

    def end_step(step, carry):
        pass_on(early, step)
        pass_on(late, step - begin_late)
        bucket_round(size - 2 + step - 1)
        return carry

    late_passed = 0
    if begin_late < size - 1:
        lax.fori_loop(begin_late + 1, size - 1, both_step, 0)
        turn(early)
        advance(late, size - 1 - begin_late)
        lax.fori_loop(1, begin_late, middle_step, 0)
        pass_on(early, begin_late)
        turn(late)
        bucket_round(size - 2 + begin_late - 1)
        lax.fori_loop(begin_late + 1, size - 1, end_step, 0)
        late_passed = size - 2 - begin_late
    else:
        lax.fori_loop(1, size - 1, middle_step, 0)
        turn(late)
    if size == 2:
        lax.fori_loop(0, units, bucket_unit, 0)

    features = gain_refs[0].shape[1]
    per_gain = features // LANES
    gain_rows = len(gain_refs) * per_gain
    small_ref[...] = jnp.zeros_like(small_ref)
    for i, ref in enumerate(gain_refs):
        total = jnp.sum(ref[...], axis=0, keepdims=True)
        for c in range(per_gain):
            at = i * per_gain + c
            small_ref[at : at + 1, :] = total[:, c * LANES : (c + 1) * LANES]
    for r in range(rows_used):
        block_sums = bucket_ref[r].reshape(LANES, LANES).T
        at = gain_rows + r
        small_ref[at : at + 1, :] = jnp.sum(block_sums, axis=0, keepdims=True)

    def near_copy(t):
        return remote(
            small_ref,
            near_ref.at[row],
            small_sems.at[0, t],
            small_sems.at[1, t],
            (me, (row + t) % peers),
        )

    def far_copy(t):
        return remote(
            far_ref.at[me],
            far_ref.at[me],
            small_sems.at[2, t],
            small_sems.at[3, t],
            ((me + t) % size, row),
        )

    for t in range(1, peers):
        near_copy(t).start()
    near_ref[pl.ds(row, 1)] = small_ref[...][None]
    for t in range(1, peers):
        near_copy(t).wait_recv()
    own = rows_used // peers
    total, sums = None, None
    for k in range(peers):
        gains = near_ref[k, :gain_rows]
        mine = near_ref[k, pl.ds(gain_rows + own * share_place(row, k, peers), own)]
        total = gains if total is None else total + gains
        sums = mine if sums is None else sums + mine
    small_ref_rows = far_ref.shape[1]
    far_ref[pl.ds(me, 1)] = jnp.concatenate(
        [total, sums, jnp.zeros((small_ref_rows - gain_rows - own, LANES), F32)], axis=0
    )[None]

    def far_start(t, carry):
        far_copy(t).start()
        return carry

    lax.fori_loop(1, size, far_start, 0)

    def late_step(step, carry):
        pass_on(late, step)
        return carry

    lax.fori_loop(1 + late_passed, size - 1, late_step, 0)

    def far_wait(t, carry):
        far_copy(t).wait()
        return carry

    lax.fori_loop(1, size, far_wait, 0)

    def far_add(k, total):
        return total + far_ref[k]

    small_out_ref[...] = lax.fori_loop(1, size, far_add, far_ref[0])
    for i, way in ready + early + late:
        out_copy(i, way, size - 2).wait_recv()

    for t in range(1, peers):
        near_copy(t).wait_send()
    if other_chip is not None:
        other_chip.wait_send()
    for i, way in early + late:
        first_copy(i, way).wait_send()

    def sent(step, carry):
        for i, way in early + late:
            next_copy(i, way, step).wait_send()
        return carry

    lax.fori_loop(1, size - 1, sent, 0)

    def sent_out(step, carry):
        for i, way in ready + early + late:
            out_copy(i, way, step).wait_send()
        return carry

    lax.fori_loop(0, size - 1, sent_out, 0)


def tail_sums(size, peers, buckets, heads, blocks, terms, last, ids, ds, gains):
    assert peers in (2, 4)
    grain = 2 * 16 * size
    features = last[0].shape[1]
    rows = [size * 2 * b.shape[1] for b in blocks]
    rows += [arrays[0].shape[0] for arrays in terms]
    rows.append(last[0].shape[0])
    padded = [r + -r % grain for r in rows]
    parts = [[b] for b in blocks]
    for arrays, r, p in zip(terms, rows[len(blocks) :], padded[len(blocks) :]):
        parts.append([jnp.pad(a, ((0, p - r), (0, 0))) for a in arrays])
    flat = [a for arrays in parts for a in arrays]
    lines = peers * (-(-heads * buckets // LANES))
    small = len(gains) * features // LANES + lines
    small = shape((small + -small % 8, LANES), F32)
    vmem, hbm = pl.BlockSpec(memory_space=pltpu.VMEM), pl.BlockSpec(memory_space=pl.ANY)
    steps = pltpu.SemaphoreType.DMA((len(rows), 2, size - 1))

    def ring_slots(i, steps):
        if i < len(blocks):
            return pltpu.VMEM((2, 1, 16, LANES), BF16)
        return pltpu.VMEM((2, *steps, padded[i] // (2 * size), features), BF16)

    *sums, small = pl.pallas_call(
        functools.partial(
            tail_kernel, size, peers, buckets, heads, len(blocks), [len(a) for a in parts]
        ),
        in_specs=[
            *[vmem] * (len(flat) + 1),
            *[hbm] * (len(last) - 1),
            vmem,
            hbm,
            *[vmem] * len(gains),
        ],
        out_specs=[vmem] * (len(rows) + 1),
        out_shape=[*[shape((p, features), BF16) for p in padded], small],
        scratch_shapes=[
            *[ring_slots(i, (size - 1,)) for i in range(len(rows))],
            *[ring_slots(i, ()) for i in range(len(rows))],
            pltpu.VMEM((rows[-1], features), BF16),
            pltpu.VMEM((padded[-1], features), BF16),
            pltpu.VMEM(ds.shape, BF16),
            pltpu.VMEM((lines, LANES // buckets, buckets, LANES), F32),
            pltpu.VMEM(small.shape, F32),
            pltpu.VMEM((peers, *small.shape), F32),
            pltpu.VMEM((size, *small.shape), F32),
            steps,
            steps,
            steps,
            steps,
            pltpu.SemaphoreType.DMA((4, max(size, peers))),
            pltpu.SemaphoreType.DMA((2,)),
            pltpu.SemaphoreType.DMA((1,)),
        ],
        compiler_params=pltpu.CompilerParams(
            vmem_limit_bytes=VMEM_BYTES, collective_id=0, has_side_effects=True
        ),
        cost_estimate=cost(),
        name="tail_sums",
    )(*flat, *last, ids, ds, *gains)
    return [total[:r] for total, r in zip(sums, rows)], small


def swap(array, bit, size):
    return lax.ppermute(array, "mp", [(i, i ^ bit) for i in range(size)])


def after(array, *others):
    return lax.optimization_barrier((array, others))[0]


def shards(
    decoder_rows,
    memory_rows,
    decoder_token_length,
    memory_length,
    bucket_ids,
    relative_bucket_bias,
    self_gain,
    self_query,
    self_key,
    self_value,
    self_out,
    cross_gain,
    cross_query,
    cross_key,
    cross_value,
    cross_out,
    hidden_gain,
    widen_weight,
    narrow_weight,
    layer_cotangent,
):
    dp_size = lax.axis_size("dp")
    mp_size = lax.axis_size("mp")
    me = lax.axis_index("mp")
    doc, features = decoder_rows.shape
    slots = memory_rows.shape[0]
    cols = self_query.shape[1]
    heads = cols // HEAD_DIM
    buckets = relative_bucket_bias.shape[0]
    order = [*range(1, mp_size, 2), *range(0, mp_size, 2)]

    doc_length = lax.dynamic_index_in_dim(decoder_token_length, me, keepdims=False)
    doc_memory = lax.dynamic_index_in_dim(memory_length, me)
    position = jnp.arange(doc, dtype=jnp.int32)
    allowed = (position[:, None] <= position[None, :]) & (position[:, None] < doc_length)
    ids = jnp.where(allowed, bucket_ids.T, buckets)
    own_self = pack(
        (self_query.T, False),
        (self_key.T, False),
        (self_value.T, False),
        (self_out, False),
        (relative_bucket_bias.T, False),
    )
    own_cross = pack(
        (cross_query.T, False), (cross_key.T, False), (cross_value.T, False), (cross_out, False)
    )
    own_hidden = pack((widen_weight, True), (narrow_weight, False))

    def first_hops(own):
        shares, bit = {0: own}, mp_size // 2
        while bit > 1:
            for j in list(shares):
                shares[j | bit] = swap(shares[j], bit, mp_size)
            bit //= 2
        return shares

    def last_hop(shares, *others):
        if 1 not in shares:
            shares[1] = swap(shares[0], 1, mp_size)
        for j in range(2, mp_size, 2):
            shares[j] = after(shares[j], *others)
            shares[j | 1] = swap(shares[j], 1, mp_size)
        return shares

    near_self = first_hops(own_self)
    near_self[1] = swap(own_self, 1, mp_size)
    memory_rows = after(memory_rows, own_self)
    w_self = last_hop(near_self, own_cross, own_hidden, ids)
    w_self = [w_self[j] for j in order]
    near_cross = first_hops(own_cross)
    near_hidden = first_hops(own_hidden)
    near_hidden[1] = swap(own_hidden, 1, mp_size)
    memory_seen = lax.all_to_all(
        memory_rows.reshape(dp_size, slots // dp_size, features), "dp", 0, 0
    ).reshape(slots, features)

    gain_self = self_gain.astype(F32)[None]
    gain_cross = cross_gain.astype(F32)[None]
    gain_hidden = hidden_gain.astype(F32)[None]

    *saved_self, after_self = self_forward(heads, buckets, decoder_rows, gain_self, w_self, ids)
    w_cross = last_hop(near_cross, after_self)
    w_cross = [w_cross[j] for j in order]
    *saved_cross, after_cross = cross_forward(
        heads, after_self, gain_cross, memory_seen, doc_memory, w_cross
    )

    before, wide_sums, narrow_sums, w_hidden = (), [], [], near_hidden
    for j in range(0, mp_size, 2):
        wide_sum, narrow_sum, *before = feed_forward(
            after_cross,
            gain_hidden,
            layer_cotangent,
            [w_hidden[j + 1], w_hidden[j]],
            before,
            j == mp_size - 2,
        )
        wide_sums.append(wide_sum)
        narrow_sums.append(narrow_sum)
        if j == 0:
            w_hidden = last_hop(near_hidden, before[0])
    layer_output, grad_after_cross, branch, hidden_gain_grad = before

    scattered, hops = wide_sums, narrow_sums[1:]
    if wide_sums[0].shape[0] % (2 * 16 * dp_size):
        scattered, hops = [], wide_sums[1:] + narrow_sums[1:]
    *sums, grad_memory, grad_after_self, branch, cross_gain_grad = cross_backward(
        heads,
        dp_size,
        after_self,
        gain_cross,
        memory_seen,
        doc_memory,
        branch,
        grad_after_cross,
        saved_cross,
        w_cross,
        scattered,
        hops,
    )
    came, sums = sums[: len(hops)], sums[len(hops) :]
    if scattered:
        blocks, terms, cross_sums = sums[:1], [narrow_sums[:1] + came], sums[1:]
    else:
        blocks, cross_sums = [], sums
        hidden = [wide_sums[0], narrow_sums[0]], came
        terms = [[jnp.concatenate(both, axis=0) for both in hidden if both]]
    memory_grad = lax.all_to_all(
        grad_memory.reshape(dp_size, slots // dp_size, features), "dp", 0, 0
    ).reshape(slots, features)

    *sums, score_grads, input_grad, self_gain_grad = self_backward(
        heads,
        decoder_rows,
        gain_self,
        branch,
        grad_after_self,
        saved_self,
        w_self,
        cross_sums[1:],
    )
    cross_sums[1:], last = sums[: len(cross_sums) - 1], sums[len(cross_sums) - 1 :]
    (*hidden, sum_cross, sum_self), small = tail_sums(
        dp_size,
        mp_size,
        buckets,
        heads,
        blocks,
        terms + [cross_sums],
        last,
        ids,
        score_grads,
        (self_gain_grad, cross_gain_grad, hidden_gain_grad),
    )
    wide_grad, narrow_grad, self_grads, cross_grads = finish(
        *(hidden if scattered else jnp.split(hidden[0], 2)), sum_cross, sum_self
    )
    gain_rows = 3 * features // LANES
    gains = small[:gain_rows].reshape(3, features)
    lines = -(-heads * buckets // LANES)
    sums = small[gain_rows : gain_rows + lines, : heads // lines * buckets]
    position_grad = sums.reshape(heads, buckets).T

    return (
        layer_output,
        input_grad,
        memory_grad,
        position_grad,
        gains[0],
        *[grad.T for grad in self_grads[:3]],
        self_grads[3],
        gains[1],
        *[grad.T for grad in cross_grads[:3]],
        cross_grads[3],
        gains[2],
        wide_grad,
        narrow_grad,
    )


def solution(mesh):
    return jax.shard_map(
        shards,
        mesh=mesh,
        in_specs=(
            P(("dp", "mp"), None),
            P(("dp", "mp"), None),
            P("dp"),
            P("dp"),
            P(),
            P(None, "mp"),
            P(),
            P(None, "mp"),
            P(None, "mp"),
            P(None, "mp"),
            P("mp", None),
            P(),
            P(None, "mp"),
            P(None, "mp"),
            P(None, "mp"),
            P("mp", None),
            P(),
            P(None, "mp"),
            P("mp", None),
            P(("dp", "mp"), None),
        ),
        out_specs=(
            P(("dp", "mp"), None),
            P(("dp", "mp"), None),
            P(("dp", "mp"), None),
            P(None, "mp"),
            P(),
            P(None, "mp"),
            P(None, "mp"),
            P(None, "mp"),
            P("mp", None),
            P(),
            P(None, "mp"),
            P(None, "mp"),
            P(None, "mp"),
            P("mp", None),
            P(),
            P(None, "mp"),
            P("mp", None),
        ),
        check_vma=False,
    )
```

profile of v0, /device:TPU:0, one launch (start us, length us, event | category | flops | bytes accessed | tf_op | source)
XLA Modules:
  0.0 361.9 jit_solution(11498168063035134479)
XLA Ops:
  0.7 2.3 pack.3.refs_2_.refs_12_
  3.0 7.4 %all-to-all-start = ((bf16[8,192,768]{2,1,0:T(8,128)(2,1)}), bf16[8,192,768]{2,1,0:T(8,128)(2,1)S(1)}, u32[]{:S(2)}, u32[]{:S(2)}) async-start(bf16[8,192,768]{2,1,0:T(8,128)(2,1)} %bitcast.30), calls=%async_computation | async-start | bytes 4718592 | tf_op jit(solution)/shard_map/all_to_all | solution.py:1697
  10.4 1.6 collective-permute-start.1
  12.0 1.3 copy.37
  13.9 3.4 pack.5.refs_1_
  17.3 2.5 pack.4.refs_2_.refs_12_
  19.8 0.7 iota_compare_fusion.1
  20.5 1.1 bitcast_select_fusion.ids_ref.refs_7_
  21.7 17.1 %collective-permute-done.1.refs_3_.refs_13_ = bf16[784,768]{1,0:T(8,128)(2,1)} collective-permute-done((bf16[784,768]{1,0:T(8,128)(2,1)}, bf16[784,768]{1,0:T(8,128)(2,1)}, u32[]{:S(2)}, u32[]{:S(2)}) %collective-permute-start.1) | collective-permute-done | bytes 1204256 | tf_op jit(solution)/shard_map/ppermute | solution.py:1617
  38.8 1.5 collective-permute-start.4
  41.9 1.1 copy-done.2
  42.9 17.7 %self_forward.1 = (bf16[512,768]{1,0:T(8,128)(2,1)}, bf16[512,768]{1,0:T(8,128)(2,1)}, bf16[512,768]{1,0:T(8,128)(2,1)}, bf16[512,768]{1,0:T(8,128)(2,1)}, f32[3...) custom-call(bf16[512,768]{1,0:T(8,128)(2,1)} %refs_0_.3, f32[1,768]{1,0:T(1,128)} %reshape.66.gain_ref.refs_1_, ...), custom_call_target="tpu_custom_call" | custom-call | flops 1048576 | bytes 65536 | tf_op jit(solution)/shard_map/self_forward/pallas_call | solution.py:958
  60.6 6.9 %collective-permute-done.4.refs_3_.refs_13_ = bf16[768,768]{1,0:T(8,128)(2,1)S(1)} collective-permute-done((bf16[768,768]{1,0:T(8,128)(2,1)S(1)}, bf16[768,768]{1,0:T(8,128)(2,1)S(1)}, u32[]{:S(2)}, u32[]{:S(2)}) %collective-permute-start.4) | collective-permute-done | bytes 1179680 | tf_op jit(solution)/shard_map/ppermute | solution.py:1617
  67.5 0.7 dynamic_slice.8.length_ref
  69.4 1.0 copy-done.4
  70.5 1.4 copy-done
  71.9 23.9 %cross_forward.1 = (bf16[512,768]{1,0:T(8,128)(2,1)}, bf16[1536,768]{1,0:T(8,128)(2,1)}, bf16[1536,768]{1,0:T(8,128)(2,1)}, bf16[512,768]{1,0:T(8,128)(2,1)}, f32[3,8,512]{2,1,0:T(8,128)}, /*index=5*/f32[512,768]{1,0:T(8,128)}) custom-call(s32[1]{0:T(128)} %dynamic_slice.8.length_ref, f32[512,768]{1,0:T(8,128)} %get-tuple-element.74.rows_ref.refs_5_, ...), custom_call_target="tpu_custom_call" | custom-call | flops 1048576 | bytes 65536 | tf_op jit(solution)/shard_map/cross_forward/pallas_call | solution.py:958
  95.9 16.9 %feed_forward.2 = (bf16[768,768]{1,0:T(8,128)(2,1)}, bf16[768,768]{1,0:T(8,128)(2,1)}, f32[512,768]{1,0:T(8,128)}, f32[512,768]{1,0:T(8,128)}) custom-call(f32[512,768]{1,0:T(8,128)} %get-tuple-element.77.rows_ref, f32[1,768]{1,0:T(1,128)} %reshape.68.gain_ref, bf16[512,768]{1,0:T(8,128)(2,1)} %cotangent_ref.3, ...), custom_call_target="tpu_custom_call" | custom-call | flops 1048576 | bytes 65536 | tf_op jit(solution)/shard_map/feed_forward/pallas_call | solution.py:958
  112.8 5.0 %collective-permute-done.6.refs_1_ = bf16[1536,768]{1,0:T(8,128)(2,1)} collective-permute-done((bf16[1536,768]{1,0:T(8,128)(2,1)}, bf16[1536,768]{1,0:T(8,128)(2,1)}, u32[]{:S(2)}, u32[]{:S(2)}) %collective-permute-start.6) | collective-permute-done | bytes 2359328 | tf_op jit(solution)/shard_map/ppermute | solution.py:1617
  117.8 4.7 %collective-permute-done.8.refs_0_ = bf16[1536,768]{1,0:T(8,128)(2,1)S(1)} collective-permute-done((bf16[1536,768]{1,0:T(8,128)(2,1)}, bf16[1536,768]{1,0:T(8,128)(2,1)S(1)}, u32[]{:S(2)}, u32[]{:S(2)}) %collective-permute-start.8) | collective-permute-done | bytes 2359328 | tf_op jit(solution)/shard_map/ppermute | solution.py:1617
  122.6 1.4 copy-done.6
  124.0 17.6 %feed_forward.3 = (bf16[768,768]{1,0:T(8,128)(2,1)}, bf16[768,768]{1,0:T(8,128)(2,1)}, bf16[512,768]{1,0:T(8,128)(2,1)}, f32[512,768]{1,0:T(8,128)}, bf16[512,768]{1,0:T(8,128)(2,1)}, /*index=5*/f32[8,768]{1,0:T(8,128)}) custom-call(f32[512,768]{1,0:T(8,128)} %get-tuple-element.77.rows_ref, f32[1,768]{1,0:T(1,128)} %reshape.68.gain_ref, ...), custom_call_target="tpu_custom_call" | custom-call | flops 1048576 | bytes 65536 | tf_op jit(solution)/shard_map/feed_forward/pallas_call | solution.py:958
  141.6 56.7 %cross_backward.1 = (bf16[768,768]{1,0:T(8,128)(2,1)}, bf16[2,48,768]{2,1,0:T(8,128)(2,1)}, bf16[768,768]{1,0:T(8,128)(2,1)}, bf16[768,768]{1,0:T(8,128)(2,1)}, ...) custom-call(s32[1]{0:T(128)} %dynamic_slice.8.length_ref, ...), custom_call_target="tpu_custom_call" | custom-call | flops 1048576 | bytes 65536 | tf_op jit(solution)/shard_map/cross_backward/pallas_call | solution.py:958
  198.3 3.9 %all-to-all-start.1 = ((bf16[8,192,768]{2,1,0:T(8,128)(2,1)}), bf16[8,192,768]{2,1,0:T(8,128)(2,1)S(1)}, u32[]{:S(2)}, u32[]{:S(2)}) async-start(bf16[8,192,768]{2,1,0:T(8,128)(2,1)} %bitcast.31), calls=%async_computation.1 | async-start | bytes 4718592 | tf_op jit(solution)/shard_map/all_to_all | solution.py:1752
  202.2 34.7 %self_backward.1 = (bf16[768,768]{1,0:T(8,128)(2,1)}, bf16[768,768]{1,0:T(8,128)(2,1)}, bf16[768,768]{1,0:T(8,128)(2,1)}, bf16[12,512,512]{2,1,0:T(8,128)(2,1)}, f32[512,768]{1,0:T(8,128)}, /*index=5*/f32[8,768]{1,0:T(8,128)}) custom-call(bf16[512,768]{1,0:T(8,128)(2,1)} %refs_0_.3, f32[1,768]{1,0:T(1,128)} %reshape.66.gain_ref.refs_1_, ...), custom_call_target="tpu_custom_call" | custom-call | flops 1048576 | bytes 65536 | tf_op jit(solution)/shard_map/self_backward/pallas_call | solution.py:958
  236.9 113.4 %tail_sums.1 = (bf16[768,768]{1,0:T(8,128)(2,1)}, bf16[768,768]{1,0:T(8,128)(2,1)}, bf16[768,768]{1,0:T(8,128)(2,1)}, bf16[768,768]{1,0:T(8,128)(2,1)}, f32[24,128]{1,0:T(8,128)}) custom-call(bf16[2,48,768]{2,1,0:T(8,128)(2,1)} %get-tuple-element.103.refs_0_, bf16[768,768]{1,0:T(8,128)(2,1)} %get-tuple-element.104.refs_1_, ...), custom_call_target="tpu_custom_call" | custom-call | flops 1048576 | bytes 65536 | tf_op jit(solution)/shard_map/tail_sums/pallas_call | solution.py:1576
  350.3 0.7 slice_reduce_fusion
  351.7 5.2 %finish.1 = (f32[768,768]{1,0:T(8,128)}, f32[768,768]{1,0:T(8,128)}, f32[192,768]{1,0:T(8,128)}, f32[192,768]{1,0:T(8,128)}, f32[192,768]{1,0:T(8,128)}, /*index...) custom-call(bf16[768,768]{1,0:T(8,128)(2,1)} %get-tuple-element.115.refs_, ...), custom_call_target="tpu_custom_call" | custom-call | flops 1048576 | bytes 65536 | tf_op jit(solution)/shard_map/finish/pallas_call | solution.py:1228
  357.5 0.9 copy.41
  358.4 0.8 copy-done.7
  359.2 1.1 copy.42
  360.3 1.4 copy.43
  (47 shorter events, 4.7 us)
Async XLA Ops:
  3.0 9.0 %copy-start.8 = (s32[512,512]{1,0:T(8,128)S(1)}, s32[512,512]{1,0:T(8,128)}, u32[]{:S(2)}) copy-start(s32[512,512]{1,0:T(8,128)} %param.24) | copy-start | bytes 3145732
  3.0 67.5 %all-to-all-start = ((bf16[8,192,768]{2,1,0:T(8,128)(2,1)}), bf16[8,192,768]{2,1,0:T(8,128)(2,1)S(1)}, u32[]{:S(2)}, u32[]{:S(2)}) async-start(bf16[8,192,768]{2,1,0:T(8,128)(2,1)} %bitcast.30), calls=%async_computation | async-start | bytes 4718592 | tf_op jit(solution)/shard_map/all_to_all | solution.py:1697
  10.4 2.9 copy-start.14
  10.4 28.3 %collective-permute-start.1 = (bf16[784,768]{1,0:T(8,128)(2,1)}, bf16[784,768]{1,0:T(8,128)(2,1)}, u32[]{:S(2)}, u32[]{:S(2)}) collective-permute-start(bf16[784,768]{1,0:T(8,128)(2,1)} %pack.3.refs_2_.refs_12_), channel_id=1, source_target_pairs={{0,2},{1,3},{2,0},{3,1},{4,6},{5,7},{6,4},{7,5},{8,10},{9,11},{10,... | collective-permute-start | bytes 3612680 | tf_op jit(solution)/shard_map/ppermute | solution.py:1617
  12.0 29.6 %collective-permute-start = (bf16[784,768]{1,0:T(8,128)(2,1)}, bf16[784,768]{1,0:T(8,128)(2,1)}, u32[]{:S(2)}, u32[]{:S(2)}) collective-permute-start(bf16[784,768]{1,0:T(8,128)(2,1)} %pack.3.refs_2_.refs_12_), channel_id=1, source_target_pairs={{0,1},{1,0},{2,3},{3,2},{4,5},{5,4},{6,7},{7,6},{8,9},{9,8},{10,11... | collective-permute-start | bytes 3612680 | tf_op jit(solution)/shard_map/ppermute | solution.py:1617
  17.3 3.2 copy-start.5
  19.8 19.0 %copy-start.1 = (bf16[768,768]{1,0:T(8,128)(2,1)S(1)}, bf16[768,768]{1,0:T(8,128)(2,1)}, u32[]{:S(2)}) copy-start(bf16[768,768]{1,0:T(8,128)(2,1)} %pack.4.refs_2_.refs_12_) | copy-start | bytes 3538948
  19.8 21.3 %copy-start.11 = (bf16[768]{0:T(1024)(128)(2,1)S(1)}, bf16[768]{0:T(1024)(128)(2,1)}, u32[]{:S(2)}) copy-start(bf16[768]{0:T(1024)(128)(2,1)} %param.26) | copy-start | bytes 4612
  38.8 3.1 collective-permute-start.2
  38.8 28.8 %collective-permute-start.4 = (bf16[768,768]{1,0:T(8,128)(2,1)S(1)}, bf16[768,768]{1,0:T(8,128)(2,1)S(1)}, u32[]{:S(2)}, u32[]{:S(2)}) collective-permute-start(bf16[768,768]{1,0:T(8,128)(2,1)S(1)} %copy-done.1), channel_id=1, source_target_pairs={{0,2},{1,3},{2,0},{3,1},{4,6},{5,7},{6,4},{7,5},{8,10},{9,11},{10,... | collective-permute-start | bytes 3538952 | tf_op jit(solution)/shard_map/ppermute | solution.py:1617
  40.3 55.6 %collective-permute-start.7 = (bf16[1536,768]{1,0:T(8,128)(2,1)}, bf16[1536,768]{1,0:T(8,128)(2,1)}, u32[]{:S(2)}, u32[]{:S(2)}) collective-permute-start(bf16[1536,768]{1,0:T(8,128)(2,1)} %pack.5.refs_1_), channel_id=1, source_target_pairs={{0,1},{1,0},{2,3},{3,2},{4,5},{5,4},{6,7},{7,6},{8,9},{9,8},{10,11... | collective-permute-start | bytes 7077896 | tf_op jit(solution)/shard_map/ppermute | solution.py:1617
  40.5 77.3 %collective-permute-start.6 = (bf16[1536,768]{1,0:T(8,128)(2,1)}, bf16[1536,768]{1,0:T(8,128)(2,1)}, u32[]{:S(2)}, u32[]{:S(2)}) collective-permute-start(bf16[1536,768]{1,0:T(8,128)(2,1)} %pack.5.refs_1_), channel_id=1, source_target_pairs={{0,2},{1,3},{2,0},{3,1},{4,6},{5,7},{6,4},{7,5},{8,10},{9,11},{10,... | collective-permute-start | bytes 7077896 | tf_op jit(solution)/shard_map/ppermute | solution.py:1617
  41.6 25.9 %copy-start.15 = (s32[4]{0:T(128)S(1)}, s32[4]{0:T(128)}, u32[]{:S(2)}) copy-start(s32[4]{0:T(128)} %param.23) | copy-start | bytes 52
  41.6 26.6 %copy-start.12 = (bf16[768]{0:T(1024)(128)(2,1)S(1)}, bf16[768]{0:T(1024)(128)(2,1)}, u32[]{:S(2)}) copy-start(bf16[768]{0:T(1024)(128)(2,1)} %param.31) | copy-start | bytes 4612
  41.6 27.2 %copy-start.13 = (bf16[768]{0:T(1024)(128)(2,1)S(1)}, bf16[768]{0:T(1024)(128)(2,1)}, u32[]{:S(2)}) copy-start(bf16[768]{0:T(1024)(128)(2,1)} %param.36) | copy-start | bytes 4612
  41.6 27.8 %collective-permute-start.3 = (bf16[768,768]{1,0:T(8,128)(2,1)S(1)}, bf16[768,768]{1,0:T(8,128)(2,1)S(1)}, u32[]{:S(2)}, u32[]{:S(2)}) collective-permute-start(bf16[768,768]{1,0:T(8,128)(2,1)S(1)} %copy-done.1), channel_id=1, source_target_pairs={{0,1},{1,0},{2,3},{3,2},{4,5},{5,4},{6,7},{7,6},{8,9},{9,8},{10,11... | collective-permute-start | bytes 3538952 | tf_op jit(solution)/shard_map/ppermute | solution.py:1617
  41.9 1.1 copy-start.2
  67.5 1.9 copy-start.3
  67.5 3.0 collective-permute-start.5
  69.4 1.0 copy-start.4
  70.5 1.4 copy-start
  117.8 4.7 %collective-permute-start.8 = (bf16[1536,768]{1,0:T(8,128)(2,1)}, bf16[1536,768]{1,0:T(8,128)(2,1)S(1)}, u32[]{:S(2)}, u32[]{:S(2)}) collective-permute-start(bf16[1536,768]{1,0:T(8,128)(2,1)} %collective-permute-done.6.refs_1_), channel_id=1, source_target_pairs={{0,1},{1,0},{2,3},{3,2},{4,5},{5,4},{6,7},{7,6},{8,9},{9,8},{10,11... | collective-permute-start | bytes 7077896 | tf_op jit(solution)/shard_map/ppermute | solution.py:1617
  122.6 1.4 copy-start.6
  198.3 159.2 %all-to-all-start.1 = ((bf16[8,192,768]{2,1,0:T(8,128)(2,1)}), bf16[8,192,768]{2,1,0:T(8,128)(2,1)S(1)}, u32[]{:S(2)}, u32[]{:S(2)}) async-start(bf16[8,192,768]{2,1,0:T(8,128)(2,1)} %bitcast.31), calls=%async_computation.1 | async-start | bytes 4718592 | tf_op jit(solution)/shard_map/all_to_all | solution.py:1752
  351.7 5.2 %copy-start.10 = (f32[24,128]{1,0:T(8,128)S(1)}, f32[24,128]{1,0:T(8,128)}, u32[]{:S(2)}) copy-start(f32[24,128]{1,0:T(8,128)} %get-tuple-element.114) | copy-start | bytes 36868
  351.7 5.8 %copy-start.9 = (bf16[512,768]{1,0:T(8,128)(2,1)S(1)}, bf16[512,768]{1,0:T(8,128)(2,1)}, u32[]{:S(2)}) copy-start(bf16[512,768]{1,0:T(8,128)(2,1)} %get-tuple-element.149) | copy-start | bytes 2359300
  357.5 1.7 copy-start.7
where the time goes:
time: 367 us; the launch traced here: 362 us
  Pallas kernels  294 us (80%)
  waiting for transfers between devices  34 us (9%)
  local copies, waits for them, and re-layouts  15.5 us (4%)
  starting transfers between devices  15.2 us (4%)
    pallas_call x6, Pallas kernels, call(): pl.pallas_call(kernel, grid=grid, in_specs=in_specs, out_specs=out_specs,...  167 us
    pallas_call x1, Pallas kernels, tail_sums(): pl.pallas_call(functools.partial(tail_kernel, size, peers, buckets, heads...  113 us
    ppermute x9, waiting for transfers between devices, swap(): return lax.ppermute(array, 'mp', [(i, i ^ bit) for i in range(size)])  34 us
    unnamed x36, local copies, waits for them, and re-layouts  10.5 us
    pallas_call x3, Pallas kernels, pack(): pl.pallas_call(functools.partial(pack_kernel, flipped), out_shape=shape((...  8.23 us
    all_to_all x1, starting transfers between devices, shards(): lax.all_to_all(memory_rows.reshape(dp_size, slots // dp_size, features),...  7.41 us
  transfers between devices with their start and end apart: 11, of which 6 were waited for; matrix products, arithmetic and copies ran while one was open for 2% of the time, Pallas kernels for 60%

commit v1 on v0

--- a/solution.py
+++ b/solution.py
@@ -763,6 +763,8 @@
         layer_in_ref,
         back_in_ref,
         product_ref,
+        even_ref,
+        odd_ref,
         sems,
         before_sems,
         swap_sems,
@@ -805,32 +807,48 @@
 
     for p, pair in enumerate(copies):
 
-        @pl.when(step == p * half)
+        @pl.when(step == max(p * half - 1, 0))
         def _(pair=pair):
             for copy in pair:
                 copy.wait()
 
-    units = pl.ds(pl.multiple_of(step * HIDDEN_BLOCK, HIDDEN_BLOCK), HIDDEN_BLOCK)
-    activated, slope = gelu_and_slope(dot_nn(wide_ref[units], normed_t[...]))
-    active_ref[units] = activated.astype(BF16)
-    grad_ref[units] = (dot_nn(narrow_ref[units], cotangent_t[...]) * slope).astype(BF16)
-
-    def store(ref, at):
-        rows = pl.ds(pl.multiple_of(at * HIDDEN_BLOCK, HIDDEN_BLOCK), HIDDEN_BLOCK)
-        ref[0, rows] = dot_nn(grad_ref[units], normed_ref[...]).astype(BF16)
-        ref[1, rows] = dot_nn(active_ref[units], cotangent_ref[...]).astype(BF16)
-
-    @pl.when(step < half)
+    def hidden_rows(block):
+        return pl.ds(pl.multiple_of(block * HIDDEN_BLOCK, HIDDEN_BLOCK), HIDDEN_BLOCK)
+
+    def products(block, target):
+        units = hidden_rows(block)
+        target[0] = dot_nn(wide_ref[units], normed_t[...])
+        target[1] = dot_nn(narrow_ref[units], cotangent_t[...])
+
+    def work(now, later, kept_in, at):
+        units = hidden_rows(step)
+        activated, slope = gelu_and_slope(now[0])
+        activated = activated.astype(BF16)
+        grad = (now[1] * slope).astype(BF16)
+        active_ref[units] = activated
+        grad_ref[units] = grad
+        products(jnp.minimum(step + 1, steps - 1), later)
+        rows = hidden_rows(at)
+        kept_in[0, rows] = dot_nn(grad, normed_ref[...]).astype(BF16)
+        kept_in[1, rows] = dot_nn(activated, cotangent_ref[...]).astype(BF16)
+
+    @pl.when(step == 0)
     def _():
-        store(give_ref, step)
+        products(0, even_ref)
+
+    for odd, (now, later) in enumerate(((even_ref, odd_ref), (odd_ref, even_ref))):
+
+        @pl.when((step % 2 == odd) & (step < half))
+        def _(now=now, later=later):
+            work(now, later, give_ref, step)
+
+        @pl.when((step % 2 == odd) & (step >= half))
+        def _(now=now, later=later):
+            work(now, later, keep_ref, step - half)
 
     @pl.when(step == half - 1)
     def _():
         swap.start()
-
-    @pl.when(step >= half)
-    def _():
-        store(keep_ref, step - half)
 
     @pl.when(step == steps - 1)
     def _():
@@ -1210,6 +1228,8 @@
             added,
             added,
             added,
+            pltpu.VMEM((2, HIDDEN_BLOCK, doc), F32),
+            pltpu.VMEM((2, HIDDEN_BLOCK, doc), F32),
             pltpu.SemaphoreType.DMA((shares, 2)),
             pltpu.SemaphoreType.DMA((2,)),
             pltpu.SemaphoreType.DMA((2,)),

time: 367 us -> 367 us (level)
  no operation moved by 1% of the time
where the time goes in v1:
time: 367 us; the launch traced here: 362 us
  Pallas kernels  294 us (80%)
  waiting for transfers between devices  34 us (9%)
  local copies, waits for them, and re-layouts  15.5 us (4%)
  starting transfers between devices  15.3 us (4%)
    pallas_call x6, Pallas kernels, call(): pl.pallas_call(kernel, grid=grid, in_specs=in_specs, out_specs=out_specs,...  167 us
    pallas_call x1, Pallas kernels, tail_sums(): pl.pallas_call(functools.partial(tail_kernel, size, peers, buckets, heads...  113 us
    ppermute x9, waiting for transfers between devices, swap(): return lax.ppermute(array, 'mp', [(i, i ^ bit) for i in range(size)])  34 us
    unnamed x36, local copies, waits for them, and re-layouts  10.5 us
    pallas_call x3, Pallas kernels, pack(): pl.pallas_call(functools.partial(pack_kernel, flipped), out_shape=shape((...  8.23 us
    all_to_all x1, starting transfers between devices, shards(): lax.all_to_all(memory_rows.reshape(dp_size, slots // dp_size, features),...  7.41 us
  transfers between devices with their start and end apart: 11, of which 6 were waited for; matrix products, arithmetic and copies ran while one was open for 2% of the time, Pallas kernels for 60%

profile of v1, /device:TPU:0, one launch (start us, length us, event | category | flops | bytes accessed | tf_op | source)
XLA Modules:
  0.0 361.9 jit_solution(18443438133038794443)
XLA Ops:
  0.7 2.3 pack.3.refs_2_.refs_12_
  3.0 7.4 %all-to-all-start = ((bf16[8,192,768]{2,1,0:T(8,128)(2,1)}), bf16[8,192,768]{2,1,0:T(8,128)(2,1)S(1)}, u32[]{:S(2)}, u32[]{:S(2)}) async-start(bf16[8,192,768]{2,1,0:T(8,128)(2,1)} %bitcast.30), calls=%async_computation | async-start | bytes 4718592 | tf_op jit(solution)/shard_map/all_to_all | solution.py:1717
  10.4 1.6 collective-permute-start.1
  12.0 1.3 copy.37
  13.9 3.4 pack.5.refs_1_
  17.3 2.5 pack.4.refs_2_.refs_12_
  19.8 0.7 iota_compare_fusion.1
  20.5 1.1 bitcast_select_fusion.ids_ref.refs_7_
  21.7 17.1 %collective-permute-done.1.refs_3_.refs_13_ = bf16[784,768]{1,0:T(8,128)(2,1)} collective-permute-done((bf16[784,768]{1,0:T(8,128)(2,1)}, bf16[784,768]{1,0:T(8,128)(2,1)}, u32[]{:S(2)}, u32[]{:S(2)}) %collective-permute-start.1) | collective-permute-done | bytes 1204256 | tf_op jit(solution)/shard_map/ppermute | solution.py:1637
  38.8 1.5 collective-permute-start.4
  41.9 1.1 copy-done.2
  42.9 17.7 %self_forward.1 = (bf16[512,768]{1,0:T(8,128)(2,1)}, bf16[512,768]{1,0:T(8,128)(2,1)}, bf16[512,768]{1,0:T(8,128)(2,1)}, bf16[512,768]{1,0:T(8,128)(2,1)}, f32[3...) custom-call(bf16[512,768]{1,0:T(8,128)(2,1)} %refs_0_.3, f32[1,768]{1,0:T(1,128)} %reshape.66.gain_ref.refs_1_, ...), custom_call_target="tpu_custom_call" | custom-call | flops 1048576 | bytes 65536 | tf_op jit(solution)/shard_map/self_forward/pallas_call | solution.py:976
  60.6 6.9 %collective-permute-done.4.refs_3_.refs_13_ = bf16[768,768]{1,0:T(8,128)(2,1)S(1)} collective-permute-done((bf16[768,768]{1,0:T(8,128)(2,1)S(1)}, bf16[768,768]{1,0:T(8,128)(2,1)S(1)}, u32[]{:S(2)}, u32[]{:S(2)}) %collective-permute-start.4) | collective-permute-done | bytes 1179680 | tf_op jit(solution)/shard_map/ppermute | solution.py:1637
  67.5 0.7 dynamic_slice.8.length_ref
  69.4 1.0 copy-done.4
  70.5 1.4 copy-done
  71.9 24.0 %cross_forward.1 = (bf16[512,768]{1,0:T(8,128)(2,1)}, bf16[1536,768]{1,0:T(8,128)(2,1)}, bf16[1536,768]{1,0:T(8,128)(2,1)}, bf16[512,768]{1,0:T(8,128)(2,1)}, f32[3,8,512]{2,1,0:T(8,128)}, /*index=5*/f32[512,768]{1,0:T(8,128)}) custom-call(s32[1]{0:T(128)} %dynamic_slice.8.length_ref, f32[512,768]{1,0:T(8,128)} %get-tuple-element.74.rows_ref.refs_5_, ...), custom_call_target="tpu_custom_call" | custom-call | flops 1048576 | bytes 65536 | tf_op jit(solution)/shard_map/cross_forward/pallas_call | solution.py:976
  95.9 16.9 %feed_forward.2 = (bf16[768,768]{1,0:T(8,128)(2,1)}, bf16[768,768]{1,0:T(8,128)(2,1)}, f32[512,768]{1,0:T(8,128)}, f32[512,768]{1,0:T(8,128)}) custom-call(f32[512,768]{1,0:T(8,128)} %get-tuple-element.77.rows_ref, f32[1,768]{1,0:T(1,128)} %reshape.68.gain_ref, bf16[512,768]{1,0:T(8,128)(2,1)} %cotangent_ref.3, ...), custom_call_target="tpu_custom_call" | custom-call | flops 1048576 | bytes 65536 | tf_op jit(solution)/shard_map/feed_forward/pallas_call | solution.py:976
  112.8 5.0 %collective-permute-done.6.refs_1_ = bf16[1536,768]{1,0:T(8,128)(2,1)} collective-permute-done((bf16[1536,768]{1,0:T(8,128)(2,1)}, bf16[1536,768]{1,0:T(8,128)(2,1)}, u32[]{:S(2)}, u32[]{:S(2)}) %collective-permute-start.6) | collective-permute-done | bytes 2359328 | tf_op jit(solution)/shard_map/ppermute | solution.py:1637
  117.8 4.7 %collective-permute-done.8.refs_0_ = bf16[1536,768]{1,0:T(8,128)(2,1)S(1)} collective-permute-done((bf16[1536,768]{1,0:T(8,128)(2,1)}, bf16[1536,768]{1,0:T(8,128)(2,1)S(1)}, u32[]{:S(2)}, u32[]{:S(2)}) %collective-permute-start.8) | collective-permute-done | bytes 2359328 | tf_op jit(solution)/shard_map/ppermute | solution.py:1637
  122.6 1.4 copy-done.6
  124.0 17.6 %feed_forward.3 = (bf16[768,768]{1,0:T(8,128)(2,1)}, bf16[768,768]{1,0:T(8,128)(2,1)}, bf16[512,768]{1,0:T(8,128)(2,1)}, f32[512,768]{1,0:T(8,128)}, bf16[512,768]{1,0:T(8,128)(2,1)}, /*index=5*/f32[8,768]{1,0:T(8,128)}) custom-call(f32[512,768]{1,0:T(8,128)} %get-tuple-element.77.rows_ref, f32[1,768]{1,0:T(1,128)} %reshape.68.gain_ref, ...), custom_call_target="tpu_custom_call" | custom-call | flops 1048576 | bytes 65536 | tf_op jit(solution)/shard_map/feed_forward/pallas_call | solution.py:976
  141.6 56.4 %cross_backward.1 = (bf16[768,768]{1,0:T(8,128)(2,1)}, bf16[2,48,768]{2,1,0:T(8,128)(2,1)}, bf16[768,768]{1,0:T(8,128)(2,1)}, bf16[768,768]{1,0:T(8,128)(2,1)}, ...) custom-call(s32[1]{0:T(128)} %dynamic_slice.8.length_ref, ...), custom_call_target="tpu_custom_call" | custom-call | flops 1048576 | bytes 65536 | tf_op jit(solution)/shard_map/cross_backward/pallas_call | solution.py:976
  198.0 4.0 %all-to-all-start.1 = ((bf16[8,192,768]{2,1,0:T(8,128)(2,1)}), bf16[8,192,768]{2,1,0:T(8,128)(2,1)S(1)}, u32[]{:S(2)}, u32[]{:S(2)}) async-start(bf16[8,192,768]{2,1,0:T(8,128)(2,1)} %bitcast.31), calls=%async_computation.1 | async-start | bytes 4718592 | tf_op jit(solution)/shard_map/all_to_all | solution.py:1772
  202.0 34.7 %self_backward.1 = (bf16[768,768]{1,0:T(8,128)(2,1)}, bf16[768,768]{1,0:T(8,128)(2,1)}, bf16[768,768]{1,0:T(8,128)(2,1)}, bf16[12,512,512]{2,1,0:T(8,128)(2,1)}, f32[512,768]{1,0:T(8,128)}, /*index=5*/f32[8,768]{1,0:T(8,128)}) custom-call(bf16[512,768]{1,0:T(8,128)(2,1)} %refs_0_.3, f32[1,768]{1,0:T(1,128)} %reshape.66.gain_ref.refs_1_, ...), custom_call_target="tpu_custom_call" | custom-call | flops 1048576 | bytes 65536 | tf_op jit(solution)/shard_map/self_backward/pallas_call | solution.py:976
  236.7 113.4 %tail_sums.1 = (bf16[768,768]{1,0:T(8,128)(2,1)}, bf16[768,768]{1,0:T(8,128)(2,1)}, bf16[768,768]{1,0:T(8,128)(2,1)}, bf16[768,768]{1,0:T(8,128)(2,1)}, f32[24,128]{1,0:T(8,128)}) custom-call(bf16[2,48,768]{2,1,0:T(8,128)(2,1)} %get-tuple-element.103.refs_0_, bf16[768,768]{1,0:T(8,128)(2,1)} %get-tuple-element.104.refs_1_, ...), custom_call_target="tpu_custom_call" | custom-call | flops 1048576 | bytes 65536 | tf_op jit(solution)/shard_map/tail_sums/pallas_call | solution.py:1596
  350.1 0.7 slice_reduce_fusion
  351.5 5.2 %finish.1 = (f32[768,768]{1,0:T(8,128)}, f32[768,768]{1,0:T(8,128)}, f32[192,768]{1,0:T(8,128)}, f32[192,768]{1,0:T(8,128)}, f32[192,768]{1,0:T(8,128)}, /*index...) custom-call(bf16[768,768]{1,0:T(8,128)(2,1)} %get-tuple-element.115.refs_, ...), custom_call_target="tpu_custom_call" | custom-call | flops 1048576 | bytes 65536 | tf_op jit(solution)/shard_map/finish/pallas_call | solution.py:1248
  357.3 0.9 copy.41
  358.1 0.8 copy-done.7
  359.0 1.1 copy.42
  360.1 1.4 copy.43
  (47 shorter events, 4.7 us)
Async XLA Ops:
  3.0 9.0 %copy-start.8 = (s32[512,512]{1,0:T(8,128)S(1)}, s32[512,512]{1,0:T(8,128)}, u32[]{:S(2)}) copy-start(s32[512,512]{1,0:T(8,128)} %param.24) | copy-start | bytes 3145732
  3.0 67.5 %all-to-all-start = ((bf16[8,192,768]{2,1,0:T(8,128)(2,1)}), bf16[8,192,768]{2,1,0:T(8,128)(2,1)S(1)}, u32[]{:S(2)}, u32[]{:S(2)}) async-start(bf16[8,192,768]{2,1,0:T(8,128)(2,1)} %bitcast.30), calls=%async_computation | async-start | bytes 4718592 | tf_op jit(solution)/shard_map/all_to_all | solution.py:1717
  10.4 2.9 copy-start.14
  10.4 28.3 %collective-permute-start.1 = (bf16[784,768]{1,0:T(8,128)(2,1)}, bf16[784,768]{1,0:T(8,128)(2,1)}, u32[]{:S(2)}, u32[]{:S(2)}) collective-permute-start(bf16[784,768]{1,0:T(8,128)(2,1)} %pack.3.refs_2_.refs_12_), channel_id=1, source_target_pairs={{0,2},{1,3},{2,0},{3,1},{4,6},{5,7},{6,4},{7,5},{8,10},{9,11},{10,... | collective-permute-start | bytes 3612680 | tf_op jit(solution)/shard_map/ppermute | solution.py:1637
  12.0 29.6 %collective-permute-start = (bf16[784,768]{1,0:T(8,128)(2,1)}, bf16[784,768]{1,0:T(8,128)(2,1)}, u32[]{:S(2)}, u32[]{:S(2)}) collective-permute-start(bf16[784,768]{1,0:T(8,128)(2,1)} %pack.3.refs_2_.refs_12_), channel_id=1, source_target_pairs={{0,1},{1,0},{2,3},{3,2},{4,5},{5,4},{6,7},{7,6},{8,9},{9,8},{10,11... | collective-permute-start | bytes 3612680 | tf_op jit(solution)/shard_map/ppermute | solution.py:1637
  17.3 3.2 copy-start.5
  19.8 19.0 %copy-start.1 = (bf16[768,768]{1,0:T(8,128)(2,1)S(1)}, bf16[768,768]{1,0:T(8,128)(2,1)}, u32[]{:S(2)}) copy-start(bf16[768,768]{1,0:T(8,128)(2,1)} %pack.4.refs_2_.refs_12_) | copy-start | bytes 3538948
  19.8 21.3 %copy-start.11 = (bf16[768]{0:T(1024)(128)(2,1)S(1)}, bf16[768]{0:T(1024)(128)(2,1)}, u32[]{:S(2)}) copy-start(bf16[768]{0:T(1024)(128)(2,1)} %param.26) | copy-start | bytes 4612
  38.8 3.1 collective-permute-start.2
  38.8 28.8 %collective-permute-start.4 = (bf16[768,768]{1,0:T(8,128)(2,1)S(1)}, bf16[768,768]{1,0:T(8,128)(2,1)S(1)}, u32[]{:S(2)}, u32[]{:S(2)}) collective-permute-start(bf16[768,768]{1,0:T(8,128)(2,1)S(1)} %copy-done.1), channel_id=1, source_target_pairs={{0,2},{1,3},{2,0},{3,1},{4,6},{5,7},{6,4},{7,5},{8,10},{9,11},{10,... | collective-permute-start | bytes 3538952 | tf_op jit(solution)/shard_map/ppermute | solution.py:1637
  40.3 55.7 %collective-permute-start.7 = (bf16[1536,768]{1,0:T(8,128)(2,1)}, bf16[1536,768]{1,0:T(8,128)(2,1)}, u32[]{:S(2)}, u32[]{:S(2)}) collective-permute-start(bf16[1536,768]{1,0:T(8,128)(2,1)} %pack.5.refs_1_), channel_id=1, source_target_pairs={{0,1},{1,0},{2,3},{3,2},{4,5},{5,4},{6,7},{7,6},{8,9},{9,8},{10,11... | collective-permute-start | bytes 7077896 | tf_op jit(solution)/shard_map/ppermute | solution.py:1637
  40.5 77.3 %collective-permute-start.6 = (bf16[1536,768]{1,0:T(8,128)(2,1)}, bf16[1536,768]{1,0:T(8,128)(2,1)}, u32[]{:S(2)}, u32[]{:S(2)}) collective-permute-start(bf16[1536,768]{1,0:T(8,128)(2,1)} %pack.5.refs_1_), channel_id=1, source_target_pairs={{0,2},{1,3},{2,0},{3,1},{4,6},{5,7},{6,4},{7,5},{8,10},{9,11},{10,... | collective-permute-start | bytes 7077896 | tf_op jit(solution)/shard_map/ppermute | solution.py:1637
  41.6 25.9 %copy-start.15 = (s32[4]{0:T(128)S(1)}, s32[4]{0:T(128)}, u32[]{:S(2)}) copy-start(s32[4]{0:T(128)} %param.23) | copy-start | bytes 52
  41.6 26.6 %copy-start.12 = (bf16[768]{0:T(1024)(128)(2,1)S(1)}, bf16[768]{0:T(1024)(128)(2,1)}, u32[]{:S(2)}) copy-start(bf16[768]{0:T(1024)(128)(2,1)} %param.31) | copy-start | bytes 4612
  41.6 27.2 %copy-start.13 = (bf16[768]{0:T(1024)(128)(2,1)S(1)}, bf16[768]{0:T(1024)(128)(2,1)}, u32[]{:S(2)}) copy-start(bf16[768]{0:T(1024)(128)(2,1)} %param.36) | copy-start | bytes 4612
  41.6 27.8 %collective-permute-start.3 = (bf16[768,768]{1,0:T(8,128)(2,1)S(1)}, bf16[768,768]{1,0:T(8,128)(2,1)S(1)}, u32[]{:S(2)}, u32[]{:S(2)}) collective-permute-start(bf16[768,768]{1,0:T(8,128)(2,1)S(1)} %copy-done.1), channel_id=1, source_target_pairs={{0,1},{1,0},{2,3},{3,2},{4,5},{5,4},{6,7},{7,6},{8,9},{9,8},{10,11... | collective-permute-start | bytes 3538952 | tf_op jit(solution)/shard_map/ppermute | solution.py:1637
  41.9 1.1 copy-start.2
  67.5 1.9 copy-start.3
  67.5 3.0 collective-permute-start.5
  69.4 1.0 copy-start.4
  70.5 1.4 copy-start
  117.8 4.7 %collective-permute-start.8 = (bf16[1536,768]{1,0:T(8,128)(2,1)}, bf16[1536,768]{1,0:T(8,128)(2,1)S(1)}, u32[]{:S(2)}, u32[]{:S(2)}) collective-permute-start(bf16[1536,768]{1,0:T(8,128)(2,1)} %collective-permute-done.6.refs_1_), channel_id=1, source_target_pairs={{0,1},{1,0},{2,3},{3,2},{4,5},{5,4},{6,7},{7,6},{8,9},{9,8},{10,11... | collective-permute-start | bytes 7077896 | tf_op jit(solution)/shard_map/ppermute | solution.py:1637
  122.6 1.4 copy-start.6
  198.0 159.3 %all-to-all-start.1 = ((bf16[8,192,768]{2,1,0:T(8,128)(2,1)}), bf16[8,192,768]{2,1,0:T(8,128)(2,1)S(1)}, u32[]{:S(2)}, u32[]{:S(2)}) async-start(bf16[8,192,768]{2,1,0:T(8,128)(2,1)} %bitcast.31), calls=%async_computation.1 | async-start | bytes 4718592 | tf_op jit(solution)/shard_map/all_to_all | solution.py:1772
  351.5 5.2 %copy-start.10 = (f32[24,128]{1,0:T(8,128)S(1)}, f32[24,128]{1,0:T(8,128)}, u32[]{:S(2)}) copy-start(f32[24,128]{1,0:T(8,128)} %get-tuple-element.114) | copy-start | bytes 36868
  351.5 5.8 %copy-start.9 = (bf16[512,768]{1,0:T(8,128)(2,1)S(1)}, bf16[512,768]{1,0:T(8,128)(2,1)}, u32[]{:S(2)}) copy-start(bf16[512,768]{1,0:T(8,128)(2,1)} %get-tuple-element.149) | copy-start | bytes 2359300
  357.3 1.7 copy-start.7

commit v2 on v0

--- a/solution.py
+++ b/solution.py
@@ -253,15 +253,20 @@
             for kind in range(kinds)
         ]
 
-    def start(self):
-        for copies in self.copies:
-            for copy in copies:
+    def start(self, *kinds):
+        for kind in kinds:
+            for copy in self.copies[kind]:
                 copy.start()
 
     def wait(self, *kinds):
         for kind in kinds:
             for copy in self.copies[kind]:
                 copy.wait()
+
+    def wait_at(self, condition, *kinds):
+        @pl.when(condition)
+        def _():
+            self.wait(*kinds)
 
 
 def table_copies(sources, tables_ref, sems, kinds):
@@ -293,22 +298,23 @@
 
     @pl.when(step == 0)
     def _():
-        stack.start()
+        stack.start(0)
         tables = table_copies(sources, tables_ref, sems, 4)
         for copy in tables:
             copy.start()
+        stack.start(1, 2, 3)
         norm_into(normed_ref, rows_ref, gain_ref)
         out_ref[...] = rows_ref[...].astype(F32)
         for copy in tables:
             copy.wait()
         table_into(table_ref, tables_ref, heads, buckets)
-        stack.wait(0, 1, 2, 3)
 
     def weights(kind):
         start = pl.multiple_of(kind * features + step * HEAD_BLOCK, HEAD_BLOCK)
         return w_ref[pl.ds(start, HEAD_BLOCK)]
 
     for kind, ref in enumerate((q_ref, k_ref, v_ref)):
+        stack.wait_at(step == 0, kind)
         ref[...] = dot_nt(normed_ref[...], weights(kind)).astype(BF16)
     none = jnp.zeros((doc, LANES), BF16)
     for pair in range(BLOCK_HEADS // 2):
@@ -329,6 +335,7 @@
                 mixed.append(dot_nn(v_t[half_rows(which), :rows], p.astype(BF16)) / total)
                 lse_ref[0, h : h + 1, span] = top + jnp.log(total)
             mixed_ref[span, lanes] = jnp.concatenate(mixed, axis=0).T.astype(BF16)
+    stack.wait_at(step == 0, 3)
     out_ref[...] += dot_nn(mixed_ref[...], weights(3))
 
 
@@ -353,7 +360,7 @@
 
     @pl.when(step == 0)
     def _():
-        stack.start()
+        stack.start(3, 0, 1, 2)
         greet([1, 2][:count])
         for hop in hops:
             hop.start()
@@ -454,7 +461,7 @@
 
     @pl.when(step == 0)
     def _():
-        stack.start()
+        stack.start(0, 1, 2, 3)
         norm_into(normed_ref, rows_ref, gain_ref)
         out_ref[...] = rows_ref[...]
         slot = lax.broadcasted_iota(jnp.int32, (slots, LANES), 0)
@@ -554,8 +561,6 @@
             pltpu.make_async_copy(source, part_ref.at[i], part_sems.at[i])
             for i, source in enumerate(scatter_in)
         ]
-        for copy in part_loads:
-            copy.start()
     sums, refs = refs[:count], refs[count:]
     memory_out, out_ref, low_ref, gain_grad_ref = refs[:4]
     rows_ref, memory_ref, add_ref, k_ref, v_ref = refs[4:9]
@@ -596,12 +601,18 @@
             for i, (source, target) in enumerate(((k_in, k_ref), (v_in, v_ref)))
         ]
 
-    stack.start()
-    for b in range(blocks):
+    stack.start(3)
+    for copy in key_copies(0):
+        copy.start()
+    if scattered:
+        for copy in part_loads:
+            copy.start()
+    for b in range(1, blocks):
         for copy in key_copies(b):
             copy.start()
     for copy in loads:
         copy.start()
+    stack.start(0, 1, 2)
     greet([1, 2][:count], [way[1] for way in ring_ways(size)] if scattered else [])
     hops = [
         to_differing(2, source, target, hop_sems.at[i])
@@ -745,10 +756,10 @@
     sources, refs = refs[:2], refs[2:]
     if not first:
         before_in, refs = refs[:2], refs[2:]
-    sums, layer_ref, out_ref = refs[:2], refs[2], refs[3]
+    outs, refs = refs[:4], refs[4:]
+    low_ref = None
     if last:
-        low_ref, gain_grad_ref = refs[4:6]
-        refs = refs[2:]
+        outs, gain_grad_ref, refs = (*outs, refs[0]), refs[1], refs[2:]
     (
         wide_ref,
         narrow_ref,
@@ -766,7 +777,16 @@
         sems,
         before_sems,
         swap_sems,
-    ) = refs[4:]
+        out_sems,
+        *results,
+    ) = refs
+    sums, (layer_ref, out_ref) = results[:2], results[2:4]
+    if last:
+        low_ref = results[4]
+    writes = [
+        pltpu.make_async_copy(source, target, out_sems.at[i])
+        for i, (source, target) in enumerate(zip(results, outs))
+    ]
     step, steps = pl.program_id(0), pl.num_programs(0)
     half = steps // 2
     doc = rows_ref.shape[0]
@@ -842,6 +862,7 @@
         for span in spans(doc, ROW_BLOCK):
             layer = rows_ref[span] if first else layer_in_ref[span]
             layer_ref[span] = (layer + product_ref[span]).astype(layer_ref.dtype)
+        writes[2].start()
         product_ref[...] = dot_tn(grad_ref[...], wide_ref[...])
         for span in spans(doc, ROW_BLOCK):
             back = product_ref[span]
@@ -853,11 +874,16 @@
                 )
             else:
                 out_ref[span] = back
+        for copy in writes[3:]:
+            copy.start()
         swap.wait_recv()
         for kind, sums_ref in enumerate(sums):
             for span in spans(hidden, HIDDEN_BLOCK):
                 sums_ref[span] = low_sum(keep_ref[kind, span], came_ref[kind, span])
+            writes[kind].start()
         swap.wait_send()
+        for copy in writes:
+            copy.wait()
 
 
 def pack_kernel(flipped, *refs):
@@ -1188,13 +1214,14 @@
     summed, tall = shape((share, features), BF16), shape((doc, features), F32)
     low = shape((doc, features), BF16)
     rest = [low, tall, low, shape((8, features), F32)] if last else [tall, tall]
+    by_copy = [summed, summed, *rest[:3]]
     kept, added = pltpu.VMEM((2, share, features), BF16), pltpu.VMEM(tall.shape, F32)
     return call(
         functools.partial(feed_forward_kernel, not before, last),
         "feed_forward",
         (steps,),
         [whole(rows), whole(gain), whole(cotangent), *anywhere(weights), *anywhere(before)],
-        (result(summed), result(summed), *[result(o) for o in rest]),
+        (*anywhere(by_copy), *[result(o) for o in rest[3:]]),
         (summed, summed, *rest),
         [
             pltpu.VMEM((hidden, features), BF16),
@@ -1213,6 +1240,8 @@
             pltpu.SemaphoreType.DMA((shares, 2)),
             pltpu.SemaphoreType.DMA((2,)),
             pltpu.SemaphoreType.DMA((2,)),
+            pltpu.SemaphoreType.DMA((len(by_copy),)),
+            *[pltpu.VMEM(o.shape, o.dtype) for o in by_copy],
         ],
         (rows, gain, cotangent, *weights, *before),
         channel=3 if before else 2,
@@ -1252,14 +1281,29 @@
 
 
 def tail_kernel(size, peers, buckets, heads, gathered, counts, *refs):
+    flat, refs = refs[: sum(counts)], refs[sum(counts) :]
+    arrays, shares = len(counts) + 1, peers // 2
+    last_refs, refs = refs[:shares], refs[shares:]
+    ids_in, ds_ref, *gain_refs = refs[:5]
+    results, small_out_ref, refs = refs[5 : 5 + arrays], refs[5 + arrays], refs[6 + arrays :]
+    outs, refs = refs[:arrays], refs[arrays:]
+    operands, refs = refs[: len(flat) + 2], refs[len(flat) + 2 :]
+    operand_sems, out_sems, refs = refs[0], refs[1], refs[2:]
+    loads = [
+        pltpu.make_async_copy(source, target, operand_sems.at[i])
+        for i, (source, target) in enumerate(zip((*flat, last_refs[0], ids_in), operands))
+    ]
+    for copy in loads:
+        copy.start()
+    last_ref, ids_ref = operands[len(flat) :]
     parts = []
     for count in counts:
-        parts.append(refs[:count])
-        refs = refs[count:]
-    arrays, shares = len(counts) + 1, peers // 2
-    last_refs, refs = refs[:shares], refs[shares:]
-    ids_ref, ds_ref, *gain_refs = refs[:5]
-    outs, small_out_ref, refs = refs[5 : 5 + arrays], refs[5 + arrays], refs[6 + arrays :]
+        parts.append(operands[:count])
+        operands = operands[count:]
+    writes = [
+        pltpu.make_async_copy(source, target, out_sems.at[i])
+        for i, (source, target) in enumerate(zip(outs, results))
+    ]
     slots, refs = refs[:arrays], refs[arrays:]
     firsts, refs = refs[:arrays], refs[arrays:]
     far_came_ref, part_ref, scores_ref, bucket_ref = refs[:4]
@@ -1372,6 +1416,8 @@
     if shares == 2:
         other_chip = to_differing(2, last_refs[1], far_came_ref, hop_sems)
         other_chip.start()
+    for copy in loads[: len(flat)]:
+        copy.wait()
     begin(early)
     for i, way in ready:
         outs[i][block(i, way, (ways[way][0] + 1) % size)] = parts[i][0][way]
@@ -1401,6 +1447,8 @@
     bucket_ref[...] = jnp.zeros_like(bucket_ref)
     part_ref[...] = jnp.zeros_like(part_ref)
     load_scores.wait()
+    for copy in loads[len(flat) :]:
+        copy.wait()
 
     def early_step(step, carry):
         advance(early, step)
@@ -1414,10 +1462,10 @@
         turn(early)
     used = slice(0, last_refs[0].shape[0])
     if other_chip is None:
-        part_ref[used] = last_refs[0][...]
+        part_ref[used] = last_ref[...]
     else:
         other_chip.wait_recv()
-        part_ref[used] = low_sum(last_refs[0][...], far_came_ref[...])
+        part_ref[used] = low_sum(last_ref[...], far_came_ref[...])
     begin(late)
 
     def both_step(step, carry):
@@ -1454,6 +1502,11 @@
     if size == 2:
         lax.fori_loop(0, units, bucket_unit, 0)
 
+    for i, way in ready + early:
+        out_copy(i, way, size - 2).wait_recv()
+        if way == 1:
+            writes[i].start()
+
     features = gain_refs[0].shape[1]
     per_gain = features // LANES
     gain_rows = len(gain_refs) * per_gain
@@ -1525,8 +1578,9 @@
         return total + far_ref[k]
 
     small_out_ref[...] = lax.fori_loop(1, size, far_add, far_ref[0])
-    for i, way in ready + early + late:
+    for i, way in late:
         out_copy(i, way, size - 2).wait_recv()
+    writes[-1].start()
 
     for t in range(1, peers):
         near_copy(t).wait_send()
@@ -1541,6 +1595,9 @@
         return carry
 
     lax.fori_loop(1, size - 1, sent, 0)
+
+    for copy in writes:
+        copy.wait()
 
     def sent_out(step, carry):
         for i, way in ready + early + late:
@@ -1578,15 +1635,16 @@
             tail_kernel, size, peers, buckets, heads, len(blocks), [len(a) for a in parts]
         ),
         in_specs=[
-            *[vmem] * (len(flat) + 1),
-            *[hbm] * (len(last) - 1),
-            vmem,
-            hbm,
+            *[hbm] * (len(flat) + len(last) + 2),
             *[vmem] * len(gains),
         ],
-        out_specs=[vmem] * (len(rows) + 1),
+        out_specs=[*[hbm] * len(rows), vmem],
         out_shape=[*[shape((p, features), BF16) for p in padded], small],
         scratch_shapes=[
+            *[pltpu.VMEM((p, features), BF16) for p in padded],
+            *[pltpu.VMEM(a.shape, a.dtype) for a in (*flat, last[0], ids)],
+            pltpu.SemaphoreType.DMA((len(flat) + 2,)),
+            pltpu.SemaphoreType.DMA((len(rows),)),
             *[ring_slots(i, (size - 1,)) for i in range(len(rows))],
             *[ring_slots(i, ()) for i in range(len(rows))],
             pltpu.VMEM((rows[-1], features), BF16),

time: 367 us -> 369 us (level)
  no operation moved by 1% of the time
where the time goes in v2:
time: 369 us; the launch traced here: 363 us
  Pallas kernels  296 us (80%)
  waiting for transfers between devices  33.4 us (9%)
  local copies, waits for them, and re-layouts  15.5 us (4%)
  starting transfers between devices  15.3 us (4%)
    pallas_call x6, Pallas kernels, call(): pl.pallas_call(kernel, grid=grid, in_specs=in_specs, out_specs=out_specs,...  168 us
    pallas_call x1, Pallas kernels, tail_sums(): pl.pallas_call(functools.partial(tail_kernel, size, peers, buckets, heads...  115 us
    ppermute x9, waiting for transfers between devices, swap(): return lax.ppermute(array, 'mp', [(i, i ^ bit) for i in range(size)])  33.4 us
    unnamed x36, local copies, waits for them, and re-layouts  10.5 us
    pallas_call x3, Pallas kernels, pack(): pl.pallas_call(functools.partial(pack_kernel, flipped), out_shape=shape((...  8.23 us
    all_to_all x1, starting transfers between devices, shards(): lax.all_to_all(memory_rows.reshape(dp_size, slots // dp_size, features),...  7.41 us
  transfers between devices with their start and end apart: 11, of which 6 were waited for; matrix products, arithmetic and copies ran while one was open for 2% of the time, Pallas kernels for 60%

profile of v2, /device:TPU:0, one launch (start us, length us, event | category | flops | bytes accessed | tf_op | source)
XLA Modules:
  0.0 363.1 jit_solution(13325030506849282046)
XLA Ops:
  0.7 2.3 pack.3.refs_2_.refs_12_
  3.0 7.4 %all-to-all-start = ((bf16[8,192,768]{2,1,0:T(8,128)(2,1)}), bf16[8,192,768]{2,1,0:T(8,128)(2,1)S(1)}, u32[]{:S(2)}, u32[]{:S(2)}) async-start(bf16[8,192,768]{2,1,0:T(8,128)(2,1)} %bitcast.30), calls=%async_computation | async-start | bytes 4718592 | tf_op jit(solution)/shard_map/all_to_all | solution.py:1755
  10.4 1.6 collective-permute-start.1
  12.0 1.3 copy.37
  13.9 3.4 pack.5.refs_1_
  17.3 2.5 pack.4.refs_2_.refs_12_
  19.8 0.7 iota_compare_fusion.1
  20.5 1.1 bitcast_select_fusion.ids_ref.refs_7_
  21.7 17.1 %collective-permute-done.1.refs_3_.refs_13_ = bf16[784,768]{1,0:T(8,128)(2,1)} collective-permute-done((bf16[784,768]{1,0:T(8,128)(2,1)}, bf16[784,768]{1,0:T(8,128)(2,1)}, u32[]{:S(2)}, u32[]{:S(2)}) %collective-permute-start.1) | collective-permute-done | bytes 1204256 | tf_op jit(solution)/shard_map/ppermute | solution.py:1675
  38.8 1.5 collective-permute-start.4
  41.9 1.1 copy-done.2
  42.9 19.1 %self_forward.1 = (bf16[512,768]{1,0:T(8,128)(2,1)}, bf16[512,768]{1,0:T(8,128)(2,1)}, bf16[512,768]{1,0:T(8,128)(2,1)}, bf16[512,768]{1,0:T(8,128)(2,1)}, f32[3...) custom-call(bf16[512,768]{1,0:T(8,128)(2,1)} %refs_0_.3, f32[1,768]{1,0:T(1,128)} %reshape.66.gain_ref.refs_1_, ...), custom_call_target="tpu_custom_call" | custom-call | flops 1048576 | bytes 65536 | tf_op jit(solution)/shard_map/self_forward/pallas_call | solution.py:984
  62.1 5.5 %collective-permute-done.4.refs_3_.refs_13_ = bf16[768,768]{1,0:T(8,128)(2,1)S(1)} collective-permute-done((bf16[768,768]{1,0:T(8,128)(2,1)S(1)}, bf16[768,768]{1,0:T(8,128)(2,1)S(1)}, u32[]{:S(2)}, u32[]{:S(2)}) %collective-permute-start.4) | collective-permute-done | bytes 1179680 | tf_op jit(solution)/shard_map/ppermute | solution.py:1675
  67.5 0.7 dynamic_slice.8.length_ref
  69.4 1.0 copy-done.4
  70.5 1.4 copy-done
  71.9 24.0 %cross_forward.1 = (bf16[512,768]{1,0:T(8,128)(2,1)}, bf16[1536,768]{1,0:T(8,128)(2,1)}, bf16[1536,768]{1,0:T(8,128)(2,1)}, bf16[512,768]{1,0:T(8,128)(2,1)}, f32[3,8,512]{2,1,0:T(8,128)}, /*index=5*/f32[512,768]{1,0:T(8,128)}) custom-call(s32[1]{0:T(128)} %dynamic_slice.8.length_ref, f32[512,768]{1,0:T(8,128)} %get-tuple-element.74.rows_ref.refs_5_, ...), custom_call_target="tpu_custom_call" | custom-call | flops 1048576 | bytes 65536 | tf_op jit(solution)/shard_map/cross_forward/pallas_call | solution.py:984
  95.9 16.0 %feed_forward.2 = (bf16[768,768]{1,0:T(8,128)(2,1)}, bf16[768,768]{1,0:T(8,128)(2,1)}, f32[512,768]{1,0:T(8,128)}, f32[512,768]{1,0:T(8,128)}) custom-call(f32[512,768]{1,0:T(8,128)} %get-tuple-element.77.rows_ref, f32[1,768]{1,0:T(1,128)} %reshape.68.gain_ref, bf16[512,768]{1,0:T(8,128)(2,1)} %cotangent_ref.3, ...), custom_call_target="tpu_custom_call" | custom-call | flops 1048576 | bytes 65536 | tf_op jit(solution)/shard_map/feed_forward/pallas_call | solution.py:984
  111.9 5.9 %collective-permute-done.6.refs_1_ = bf16[1536,768]{1,0:T(8,128)(2,1)} collective-permute-done((bf16[1536,768]{1,0:T(8,128)(2,1)}, bf16[1536,768]{1,0:T(8,128)(2,1)}, u32[]{:S(2)}, u32[]{:S(2)}) %collective-permute-start.6) | collective-permute-done | bytes 2359328 | tf_op jit(solution)/shard_map/ppermute | solution.py:1675
  117.8 4.7 %collective-permute-done.8.refs_0_ = bf16[1536,768]{1,0:T(8,128)(2,1)S(1)} collective-permute-done((bf16[1536,768]{1,0:T(8,128)(2,1)}, bf16[1536,768]{1,0:T(8,128)(2,1)S(1)}, u32[]{:S(2)}, u32[]{:S(2)}) %collective-permute-start.8) | collective-permute-done | bytes 2359328 | tf_op jit(solution)/shard_map/ppermute | solution.py:1675
  122.6 1.4 copy-done.6
  124.0 17.4 %feed_forward.3 = (bf16[768,768]{1,0:T(8,128)(2,1)}, bf16[768,768]{1,0:T(8,128)(2,1)}, bf16[512,768]{1,0:T(8,128)(2,1)}, f32[512,768]{1,0:T(8,128)}, bf16[512,768]{1,0:T(8,128)(2,1)}, /*index=5*/f32[8,768]{1,0:T(8,128)}) custom-call(f32[512,768]{1,0:T(8,128)} %get-tuple-element.77.rows_ref, f32[1,768]{1,0:T(1,128)} %reshape.68.gain_ref, ...), custom_call_target="tpu_custom_call" | custom-call | flops 1048576 | bytes 65536 | tf_op jit(solution)/shard_map/feed_forward/pallas_call | solution.py:984
  141.4 56.4 %cross_backward.1 = (bf16[768,768]{1,0:T(8,128)(2,1)}, bf16[2,48,768]{2,1,0:T(8,128)(2,1)}, bf16[768,768]{1,0:T(8,128)(2,1)}, bf16[768,768]{1,0:T(8,128)(2,1)}, ...) custom-call(s32[1]{0:T(128)} %dynamic_slice.8.length_ref, ...), custom_call_target="tpu_custom_call" | custom-call | flops 1048576 | bytes 65536 | tf_op jit(solution)/shard_map/cross_backward/pallas_call | solution.py:984
  197.8 4.0 %all-to-all-start.1 = ((bf16[8,192,768]{2,1,0:T(8,128)(2,1)}), bf16[8,192,768]{2,1,0:T(8,128)(2,1)S(1)}, u32[]{:S(2)}, u32[]{:S(2)}) async-start(bf16[8,192,768]{2,1,0:T(8,128)(2,1)} %bitcast.31), calls=%async_computation.1 | async-start | bytes 4718592 | tf_op jit(solution)/shard_map/all_to_all | solution.py:1810
  201.8 34.7 %self_backward.1 = (bf16[768,768]{1,0:T(8,128)(2,1)}, bf16[768,768]{1,0:T(8,128)(2,1)}, bf16[768,768]{1,0:T(8,128)(2,1)}, bf16[12,512,512]{2,1,0:T(8,128)(2,1)}, f32[512,768]{1,0:T(8,128)}, /*index=5*/f32[8,768]{1,0:T(8,128)}) custom-call(bf16[512,768]{1,0:T(8,128)(2,1)} %refs_0_.3, f32[1,768]{1,0:T(1,128)} %reshape.66.gain_ref.refs_1_, ...), custom_call_target="tpu_custom_call" | custom-call | flops 1048576 | bytes 65536 | tf_op jit(solution)/shard_map/self_backward/pallas_call | solution.py:984
  236.5 114.7 %tail_sums.1 = (bf16[768,768]{1,0:T(8,128)(2,1)}, bf16[768,768]{1,0:T(8,128)(2,1)}, bf16[768,768]{1,0:T(8,128)(2,1)}, bf16[768,768]{1,0:T(8,128)(2,1)}, f32[24,128]{1,0:T(8,128)}) custom-call(bf16[2,48,768]{2,1,0:T(8,128)(2,1)} %get-tuple-element.103.refs_0_, bf16[768,768]{1,0:T(8,128)(2,1)} %get-tuple-element.104.refs_1_, ...), custom_call_target="tpu_custom_call" | custom-call | flops 1048576 | bytes 65536 | tf_op jit(solution)/shard_map/tail_sums/pallas_call | solution.py:1633
  351.3 0.7 slice_reduce_fusion
  352.6 5.2 %finish.1 = (f32[768,768]{1,0:T(8,128)}, f32[768,768]{1,0:T(8,128)}, f32[192,768]{1,0:T(8,128)}, f32[192,768]{1,0:T(8,128)}, f32[192,768]{1,0:T(8,128)}, /*index...) custom-call(bf16[768,768]{1,0:T(8,128)(2,1)} %get-tuple-element.115.refs_, ...), custom_call_target="tpu_custom_call" | custom-call | flops 1048576 | bytes 65536 | tf_op jit(solution)/shard_map/finish/pallas_call | solution.py:1257
  358.4 0.9 copy.41
  359.3 0.8 copy-done.7
  360.1 1.1 copy.42
  361.3 1.4 copy.43
  (47 shorter events, 4.7 us)
Async XLA Ops:
  3.0 9.0 %copy-start.8 = (s32[512,512]{1,0:T(8,128)S(1)}, s32[512,512]{1,0:T(8,128)}, u32[]{:S(2)}) copy-start(s32[512,512]{1,0:T(8,128)} %param.24) | copy-start | bytes 3145732
  3.0 67.5 %all-to-all-start = ((bf16[8,192,768]{2,1,0:T(8,128)(2,1)}), bf16[8,192,768]{2,1,0:T(8,128)(2,1)S(1)}, u32[]{:S(2)}, u32[]{:S(2)}) async-start(bf16[8,192,768]{2,1,0:T(8,128)(2,1)} %bitcast.30), calls=%async_computation | async-start | bytes 4718592 | tf_op jit(solution)/shard_map/all_to_all | solution.py:1755
  10.4 2.9 copy-start.14
  10.4 28.3 %collective-permute-start.1 = (bf16[784,768]{1,0:T(8,128)(2,1)}, bf16[784,768]{1,0:T(8,128)(2,1)}, u32[]{:S(2)}, u32[]{:S(2)}) collective-permute-start(bf16[784,768]{1,0:T(8,128)(2,1)} %pack.3.refs_2_.refs_12_), channel_id=1, source_target_pairs={{0,2},{1,3},{2,0},{3,1},{4,6},{5,7},{6,4},{7,5},{8,10},{9,11},{10,... | collective-permute-start | bytes 3612680 | tf_op jit(solution)/shard_map/ppermute | solution.py:1675
  12.0 29.6 %collective-permute-start = (bf16[784,768]{1,0:T(8,128)(2,1)}, bf16[784,768]{1,0:T(8,128)(2,1)}, u32[]{:S(2)}, u32[]{:S(2)}) collective-permute-start(bf16[784,768]{1,0:T(8,128)(2,1)} %pack.3.refs_2_.refs_12_), channel_id=1, source_target_pairs={{0,1},{1,0},{2,3},{3,2},{4,5},{5,4},{6,7},{7,6},{8,9},{9,8},{10,11... | collective-permute-start | bytes 3612680 | tf_op jit(solution)/shard_map/ppermute | solution.py:1675
  17.3 3.2 copy-start.5
  19.8 19.0 %copy-start.1 = (bf16[768,768]{1,0:T(8,128)(2,1)S(1)}, bf16[768,768]{1,0:T(8,128)(2,1)}, u32[]{:S(2)}) copy-start(bf16[768,768]{1,0:T(8,128)(2,1)} %pack.4.refs_2_.refs_12_) | copy-start | bytes 3538948
  19.8 21.3 %copy-start.11 = (bf16[768]{0:T(1024)(128)(2,1)S(1)}, bf16[768]{0:T(1024)(128)(2,1)}, u32[]{:S(2)}) copy-start(bf16[768]{0:T(1024)(128)(2,1)} %param.26) | copy-start | bytes 4612
  38.8 3.1 collective-permute-start.2
  38.8 28.8 %collective-permute-start.4 = (bf16[768,768]{1,0:T(8,128)(2,1)S(1)}, bf16[768,768]{1,0:T(8,128)(2,1)S(1)}, u32[]{:S(2)}, u32[]{:S(2)}) collective-permute-start(bf16[768,768]{1,0:T(8,128)(2,1)S(1)} %copy-done.1), channel_id=1, source_target_pairs={{0,2},{1,3},{2,0},{3,1},{4,6},{5,7},{6,4},{7,5},{8,10},{9,11},{10,... | collective-permute-start | bytes 3538952 | tf_op jit(solution)/shard_map/ppermute | solution.py:1675
  40.3 55.7 %collective-permute-start.7 = (bf16[1536,768]{1,0:T(8,128)(2,1)}, bf16[1536,768]{1,0:T(8,128)(2,1)}, u32[]{:S(2)}, u32[]{:S(2)}) collective-permute-start(bf16[1536,768]{1,0:T(8,128)(2,1)} %pack.5.refs_1_), channel_id=1, source_target_pairs={{0,1},{1,0},{2,3},{3,2},{4,5},{5,4},{6,7},{7,6},{8,9},{9,8},{10,11... | collective-permute-start | bytes 7077896 | tf_op jit(solution)/shard_map/ppermute | solution.py:1675
  40.5 77.3 %collective-permute-start.6 = (bf16[1536,768]{1,0:T(8,128)(2,1)}, bf16[1536,768]{1,0:T(8,128)(2,1)}, u32[]{:S(2)}, u32[]{:S(2)}) collective-permute-start(bf16[1536,768]{1,0:T(8,128)(2,1)} %pack.5.refs_1_), channel_id=1, source_target_pairs={{0,2},{1,3},{2,0},{3,1},{4,6},{5,7},{6,4},{7,5},{8,10},{9,11},{10,... | collective-permute-start | bytes 7077896 | tf_op jit(solution)/shard_map/ppermute | solution.py:1675
  41.6 25.9 %copy-start.15 = (s32[4]{0:T(128)S(1)}, s32[4]{0:T(128)}, u32[]{:S(2)}) copy-start(s32[4]{0:T(128)} %param.23) | copy-start | bytes 52
  41.6 26.6 %copy-start.12 = (bf16[768]{0:T(1024)(128)(2,1)S(1)}, bf16[768]{0:T(1024)(128)(2,1)}, u32[]{:S(2)}) copy-start(bf16[768]{0:T(1024)(128)(2,1)} %param.31) | copy-start | bytes 4612
  41.6 27.2 %copy-start.13 = (bf16[768]{0:T(1024)(128)(2,1)S(1)}, bf16[768]{0:T(1024)(128)(2,1)}, u32[]{:S(2)}) copy-start(bf16[768]{0:T(1024)(128)(2,1)} %param.36) | copy-start | bytes 4612
  41.6 27.8 %collective-permute-start.3 = (bf16[768,768]{1,0:T(8,128)(2,1)S(1)}, bf16[768,768]{1,0:T(8,128)(2,1)S(1)}, u32[]{:S(2)}, u32[]{:S(2)}) collective-permute-start(bf16[768,768]{1,0:T(8,128)(2,1)S(1)} %copy-done.1), channel_id=1, source_target_pairs={{0,1},{1,0},{2,3},{3,2},{4,5},{5,4},{6,7},{7,6},{8,9},{9,8},{10,11... | collective-permute-start | bytes 3538952 | tf_op jit(solution)/shard_map/ppermute | solution.py:1675
  41.9 1.1 copy-start.2
  67.5 1.9 copy-start.3
  67.5 3.0 collective-permute-start.5
  69.4 1.0 copy-start.4
  70.5 1.4 copy-start
  117.8 4.7 %collective-permute-start.8 = (bf16[1536,768]{1,0:T(8,128)(2,1)}, bf16[1536,768]{1,0:T(8,128)(2,1)S(1)}, u32[]{:S(2)}, u32[]{:S(2)}) collective-permute-start(bf16[1536,768]{1,0:T(8,128)(2,1)} %collective-permute-done.6.refs_1_), channel_id=1, source_target_pairs={{0,1},{1,0},{2,3},{3,2},{4,5},{5,4},{6,7},{7,6},{8,9},{9,8},{10,11... | collective-permute-start | bytes 7077896 | tf_op jit(solution)/shard_map/ppermute | solution.py:1675
  122.6 1.4 copy-start.6
  197.8 160.6 %all-to-all-start.1 = ((bf16[8,192,768]{2,1,0:T(8,128)(2,1)}), bf16[8,192,768]{2,1,0:T(8,128)(2,1)S(1)}, u32[]{:S(2)}, u32[]{:S(2)}) async-start(bf16[8,192,768]{2,1,0:T(8,128)(2,1)} %bitcast.31), calls=%async_computation.1 | async-start | bytes 4718592 | tf_op jit(solution)/shard_map/all_to_all | solution.py:1810
  352.6 5.2 %copy-start.10 = (f32[24,128]{1,0:T(8,128)S(1)}, f32[24,128]{1,0:T(8,128)}, u32[]{:S(2)}) copy-start(f32[24,128]{1,0:T(8,128)} %get-tuple-element.114) | copy-start | bytes 36868
  352.6 5.8 %copy-start.9 = (bf16[512,768]{1,0:T(8,128)(2,1)S(1)}, bf16[512,768]{1,0:T(8,128)(2,1)}, u32[]{:S(2)}) copy-start(bf16[512,768]{1,0:T(8,128)(2,1)} %get-tuple-element.149) | copy-start | bytes 2359300
  358.4 1.7 copy-start.7

commit v3 on v0

--- a/solution.py
+++ b/solution.py
@@ -18,6 +18,8 @@
 TILE_ROWS = 16
 LARGEST_SUM = 1e30
 LATE_STEP = 4
+UNIT_BUCKETS = 4
+UNIT_ROWS = 64
 HEAD_BLOCK = 256
 BLOCK_HEADS = HEAD_BLOCK // HEAD_DIM
 Q_BLOCK = 256
@@ -1378,20 +1380,28 @@
         out_copy(i, way, 0).start()
 
     rows_used, per_row = bucket_ref.shape[0], ds_ref.shape[0] // bucket_ref.shape[0]
-    units = rows_used * buckets
+    per_line = buckets // UNIT_BUCKETS
+    units = rows_used * per_line
     per_round = -(-units // max(2 * (size - 2), 1))
 
     def bucket_unit(u, carry):
-        r, b = u // buckets, u % buckets
-        sums = [jnp.zeros((8, LANES), F32) for _ in range(per_row)]
+        r, first = u // per_line, u % per_line * UNIT_BUCKETS
+        sums = [[jnp.zeros((8, LANES), F32)] * UNIT_BUCKETS for _ in range(per_row)]
         for c in range(0, doc, LANES):
-            hit = ids_ref[: c + LANES, c : c + LANES] == b
-            for h in range(per_row):
-                grads = scores_ref[r * per_row + h, : c + LANES, c : c + LANES].astype(F32)
-                kept = jnp.where(hit, grads, 0.0).reshape(-1, 8, LANES)
-                sums[h] = sums[h] + jnp.sum(kept, axis=0)
+            lanes = slice(c, c + LANES)
+            for rows in spans(c + LANES, UNIT_ROWS):
+                found = ids_ref[rows, lanes] - first
+                hits = [found == b for b in range(UNIT_BUCKETS)]
+                for h in range(per_row):
+                    grads = scores_ref[r * per_row + h, rows, lanes].astype(F32)
+                    for b, hit in enumerate(hits):
+                        kept = jnp.where(hit, grads, 0.0).reshape(-1, 8, LANES)
+                        sums[h][b] = sums[h][b] + jnp.sum(kept, axis=0)
         for h in range(per_row):
-            bucket_ref[r, h, pl.ds(b, 1), :] = jnp.sum(sums[h], axis=0, keepdims=True)
+            for b in range(UNIT_BUCKETS):
+                bucket_ref[r, h, pl.ds(first + b, 1), :] = jnp.sum(
+                    sums[h][b], axis=0, keepdims=True
+                )
         return carry
 
     def bucket_round(k):

time: 367 us -> 365 us (level)
  no operation moved by 1% of the time
where the time goes in v3:
time: 365 us; the launch traced here: 359 us
  Pallas kernels  292 us (80%)
  waiting for transfers between devices  34 us (9%)
  local copies, waits for them, and re-layouts  15.5 us (4%)
  starting transfers between devices  15.2 us (4%)
    pallas_call x6, Pallas kernels, call(): pl.pallas_call(kernel, grid=grid, in_specs=in_specs, out_specs=out_specs,...  167 us
    pallas_call x1, Pallas kernels, tail_sums(): pl.pallas_call(functools.partial(tail_kernel, size, peers, buckets, heads...  111 us
    ppermute x9, waiting for transfers between devices, swap(): return lax.ppermute(array, 'mp', [(i, i ^ bit) for i in range(size)])  34 us
    unnamed x36, local copies, waits for them, and re-layouts  10.5 us
    pallas_call x3, Pallas kernels, pack(): pl.pallas_call(functools.partial(pack_kernel, flipped), out_shape=shape((...  8.23 us
    all_to_all x1, starting transfers between devices, shards(): lax.all_to_all(memory_rows.reshape(dp_size, slots // dp_size, features),...  7.41 us
  transfers between devices with their start and end apart: 11, of which 6 were waited for; matrix products, arithmetic and copies ran while one was open for 2% of the time, Pallas kernels for 60%

profile of v3, /device:TPU:0, one launch (start us, length us, event | category | flops | bytes accessed | tf_op | source)
XLA Modules:
  0.0 359.3 jit_solution(2340428067384576422)
XLA Ops:
  0.7 2.3 pack.3.refs_2_.refs_12_
  3.0 7.4 %all-to-all-start = ((bf16[8,192,768]{2,1,0:T(8,128)(2,1)}), bf16[8,192,768]{2,1,0:T(8,128)(2,1)S(1)}, u32[]{:S(2)}, u32[]{:S(2)}) async-start(bf16[8,192,768]{2,1,0:T(8,128)(2,1)} %bitcast.30), calls=%async_computation | async-start | bytes 4718592 | tf_op jit(solution)/shard_map/all_to_all | solution.py:1707
  10.4 1.6 collective-permute-start.1
  12.0 1.3 copy.37
  13.9 3.4 pack.5.refs_1_
  17.3 2.5 pack.4.refs_2_.refs_12_
  19.8 0.7 iota_compare_fusion.1
  20.5 1.1 bitcast_select_fusion.ids_ref.refs_7_
  21.7 17.1 %collective-permute-done.1.refs_3_.refs_13_ = bf16[784,768]{1,0:T(8,128)(2,1)} collective-permute-done((bf16[784,768]{1,0:T(8,128)(2,1)}, bf16[784,768]{1,0:T(8,128)(2,1)}, u32[]{:S(2)}, u32[]{:S(2)}) %collective-permute-start.1) | collective-permute-done | bytes 1204256 | tf_op jit(solution)/shard_map/ppermute | solution.py:1627
  38.8 1.5 collective-permute-start.4
  41.9 1.1 copy-done.2
  42.9 17.6 %self_forward.1 = (bf16[512,768]{1,0:T(8,128)(2,1)}, bf16[512,768]{1,0:T(8,128)(2,1)}, bf16[512,768]{1,0:T(8,128)(2,1)}, bf16[512,768]{1,0:T(8,128)(2,1)}, f32[3...) custom-call(bf16[512,768]{1,0:T(8,128)(2,1)} %refs_0_.3, f32[1,768]{1,0:T(1,128)} %reshape.66.gain_ref.refs_1_, ...), custom_call_target="tpu_custom_call" | custom-call | flops 1048576 | bytes 65536 | tf_op jit(solution)/shard_map/self_forward/pallas_call | solution.py:960
  60.6 6.9 %collective-permute-done.4.refs_3_.refs_13_ = bf16[768,768]{1,0:T(8,128)(2,1)S(1)} collective-permute-done((bf16[768,768]{1,0:T(8,128)(2,1)S(1)}, bf16[768,768]{1,0:T(8,128)(2,1)S(1)}, u32[]{:S(2)}, u32[]{:S(2)}) %collective-permute-start.4) | collective-permute-done | bytes 1179680 | tf_op jit(solution)/shard_map/ppermute | solution.py:1627
  67.5 0.7 dynamic_slice.8.length_ref
  69.4 1.0 copy-done.4
  70.5 1.4 copy-done
  71.9 23.9 %cross_forward.1 = (bf16[512,768]{1,0:T(8,128)(2,1)}, bf16[1536,768]{1,0:T(8,128)(2,1)}, bf16[1536,768]{1,0:T(8,128)(2,1)}, bf16[512,768]{1,0:T(8,128)(2,1)}, f32[3,8,512]{2,1,0:T(8,128)}, /*index=5*/f32[512,768]{1,0:T(8,128)}) custom-call(s32[1]{0:T(128)} %dynamic_slice.8.length_ref, f32[512,768]{1,0:T(8,128)} %get-tuple-element.74.rows_ref.refs_5_, ...), custom_call_target="tpu_custom_call" | custom-call | flops 1048576 | bytes 65536 | tf_op jit(solution)/shard_map/cross_forward/pallas_call | solution.py:960
  95.9 16.9 %feed_forward.2 = (bf16[768,768]{1,0:T(8,128)(2,1)}, bf16[768,768]{1,0:T(8,128)(2,1)}, f32[512,768]{1,0:T(8,128)}, f32[512,768]{1,0:T(8,128)}) custom-call(f32[512,768]{1,0:T(8,128)} %get-tuple-element.77.rows_ref, f32[1,768]{1,0:T(1,128)} %reshape.68.gain_ref, bf16[512,768]{1,0:T(8,128)(2,1)} %cotangent_ref.3, ...), custom_call_target="tpu_custom_call" | custom-call | flops 1048576 | bytes 65536 | tf_op jit(solution)/shard_map/feed_forward/pallas_call | solution.py:960
  112.8 5.0 %collective-permute-done.6.refs_1_ = bf16[1536,768]{1,0:T(8,128)(2,1)} collective-permute-done((bf16[1536,768]{1,0:T(8,128)(2,1)}, bf16[1536,768]{1,0:T(8,128)(2,1)}, u32[]{:S(2)}, u32[]{:S(2)}) %collective-permute-start.6) | collective-permute-done | bytes 2359328 | tf_op jit(solution)/shard_map/ppermute | solution.py:1627
  117.8 4.7 %collective-permute-done.8.refs_0_ = bf16[1536,768]{1,0:T(8,128)(2,1)S(1)} collective-permute-done((bf16[1536,768]{1,0:T(8,128)(2,1)}, bf16[1536,768]{1,0:T(8,128)(2,1)S(1)}, u32[]{:S(2)}, u32[]{:S(2)}) %collective-permute-start.8) | collective-permute-done | bytes 2359328 | tf_op jit(solution)/shard_map/ppermute | solution.py:1627
  122.6 1.4 copy-done.6
  124.0 17.6 %feed_forward.3 = (bf16[768,768]{1,0:T(8,128)(2,1)}, bf16[768,768]{1,0:T(8,128)(2,1)}, bf16[512,768]{1,0:T(8,128)(2,1)}, f32[512,768]{1,0:T(8,128)}, bf16[512,768]{1,0:T(8,128)(2,1)}, /*index=5*/f32[8,768]{1,0:T(8,128)}) custom-call(f32[512,768]{1,0:T(8,128)} %get-tuple-element.77.rows_ref, f32[1,768]{1,0:T(1,128)} %reshape.68.gain_ref, ...), custom_call_target="tpu_custom_call" | custom-call | flops 1048576 | bytes 65536 | tf_op jit(solution)/shard_map/feed_forward/pallas_call | solution.py:960
  141.6 56.7 %cross_backward.1 = (bf16[768,768]{1,0:T(8,128)(2,1)}, bf16[2,48,768]{2,1,0:T(8,128)(2,1)}, bf16[768,768]{1,0:T(8,128)(2,1)}, bf16[768,768]{1,0:T(8,128)(2,1)}, ...) custom-call(s32[1]{0:T(128)} %dynamic_slice.8.length_ref, ...), custom_call_target="tpu_custom_call" | custom-call | flops 1048576 | bytes 65536 | tf_op jit(solution)/shard_map/cross_backward/pallas_call | solution.py:960
  198.3 3.9 %all-to-all-start.1 = ((bf16[8,192,768]{2,1,0:T(8,128)(2,1)}), bf16[8,192,768]{2,1,0:T(8,128)(2,1)S(1)}, u32[]{:S(2)}, u32[]{:S(2)}) async-start(bf16[8,192,768]{2,1,0:T(8,128)(2,1)} %bitcast.31), calls=%async_computation.1 | async-start | bytes 4718592 | tf_op jit(solution)/shard_map/all_to_all | solution.py:1762
  202.2 34.7 %self_backward.1 = (bf16[768,768]{1,0:T(8,128)(2,1)}, bf16[768,768]{1,0:T(8,128)(2,1)}, bf16[768,768]{1,0:T(8,128)(2,1)}, bf16[12,512,512]{2,1,0:T(8,128)(2,1)}, f32[512,768]{1,0:T(8,128)}, /*index=5*/f32[8,768]{1,0:T(8,128)}) custom-call(bf16[512,768]{1,0:T(8,128)(2,1)} %refs_0_.3, f32[1,768]{1,0:T(1,128)} %reshape.66.gain_ref.refs_1_, ...), custom_call_target="tpu_custom_call" | custom-call | flops 1048576 | bytes 65536 | tf_op jit(solution)/shard_map/self_backward/pallas_call | solution.py:960
  236.9 110.8 %tail_sums.1 = (bf16[768,768]{1,0:T(8,128)(2,1)}, bf16[768,768]{1,0:T(8,128)(2,1)}, bf16[768,768]{1,0:T(8,128)(2,1)}, bf16[768,768]{1,0:T(8,128)(2,1)}, f32[24,128]{1,0:T(8,128)}) custom-call(bf16[2,48,768]{2,1,0:T(8,128)(2,1)} %get-tuple-element.103.refs_0_, bf16[768,768]{1,0:T(8,128)(2,1)} %get-tuple-element.104.refs_1_, ...), custom_call_target="tpu_custom_call" | custom-call | flops 1048576 | bytes 65536 | tf_op jit(solution)/shard_map/tail_sums/pallas_call | solution.py:1586
  347.7 0.7 slice_reduce_fusion
  349.0 5.2 %finish.1 = (f32[768,768]{1,0:T(8,128)}, f32[768,768]{1,0:T(8,128)}, f32[192,768]{1,0:T(8,128)}, f32[192,768]{1,0:T(8,128)}, f32[192,768]{1,0:T(8,128)}, /*index...) custom-call(bf16[768,768]{1,0:T(8,128)(2,1)} %get-tuple-element.115.refs_, ...), custom_call_target="tpu_custom_call" | custom-call | flops 1048576 | bytes 65536 | tf_op jit(solution)/shard_map/finish/pallas_call | solution.py:1230
  354.8 0.9 copy.41
  355.7 0.8 copy-done.7
  356.5 1.1 copy.42
  357.6 1.4 copy.43
  (47 shorter events, 4.7 us)
Async XLA Ops:
  3.0 9.0 %copy-start.8 = (s32[512,512]{1,0:T(8,128)S(1)}, s32[512,512]{1,0:T(8,128)}, u32[]{:S(2)}) copy-start(s32[512,512]{1,0:T(8,128)} %param.24) | copy-start | bytes 3145732
  3.0 67.5 %all-to-all-start = ((bf16[8,192,768]{2,1,0:T(8,128)(2,1)}), bf16[8,192,768]{2,1,0:T(8,128)(2,1)S(1)}, u32[]{:S(2)}, u32[]{:S(2)}) async-start(bf16[8,192,768]{2,1,0:T(8,128)(2,1)} %bitcast.30), calls=%async_computation | async-start | bytes 4718592 | tf_op jit(solution)/shard_map/all_to_all | solution.py:1707
  10.4 2.9 copy-start.14
  10.4 28.3 %collective-permute-start.1 = (bf16[784,768]{1,0:T(8,128)(2,1)}, bf16[784,768]{1,0:T(8,128)(2,1)}, u32[]{:S(2)}, u32[]{:S(2)}) collective-permute-start(bf16[784,768]{1,0:T(8,128)(2,1)} %pack.3.refs_2_.refs_12_), channel_id=1, source_target_pairs={{0,2},{1,3},{2,0},{3,1},{4,6},{5,7},{6,4},{7,5},{8,10},{9,11},{10,... | collective-permute-start | bytes 3612680 | tf_op jit(solution)/shard_map/ppermute | solution.py:1627
  12.0 29.6 %collective-permute-start = (bf16[784,768]{1,0:T(8,128)(2,1)}, bf16[784,768]{1,0:T(8,128)(2,1)}, u32[]{:S(2)}, u32[]{:S(2)}) collective-permute-start(bf16[784,768]{1,0:T(8,128)(2,1)} %pack.3.refs_2_.refs_12_), channel_id=1, source_target_pairs={{0,1},{1,0},{2,3},{3,2},{4,5},{5,4},{6,7},{7,6},{8,9},{9,8},{10,11... | collective-permute-start | bytes 3612680 | tf_op jit(solution)/shard_map/ppermute | solution.py:1627
  17.3 3.2 copy-start.5
  19.8 19.0 %copy-start.1 = (bf16[768,768]{1,0:T(8,128)(2,1)S(1)}, bf16[768,768]{1,0:T(8,128)(2,1)}, u32[]{:S(2)}) copy-start(bf16[768,768]{1,0:T(8,128)(2,1)} %pack.4.refs_2_.refs_12_) | copy-start | bytes 3538948
  19.8 21.3 %copy-start.11 = (bf16[768]{0:T(1024)(128)(2,1)S(1)}, bf16[768]{0:T(1024)(128)(2,1)}, u32[]{:S(2)}) copy-start(bf16[768]{0:T(1024)(128)(2,1)} %param.26) | copy-start | bytes 4612
  38.8 3.1 collective-permute-start.2
  38.8 28.8 %collective-permute-start.4 = (bf16[768,768]{1,0:T(8,128)(2,1)S(1)}, bf16[768,768]{1,0:T(8,128)(2,1)S(1)}, u32[]{:S(2)}, u32[]{:S(2)}) collective-permute-start(bf16[768,768]{1,0:T(8,128)(2,1)S(1)} %copy-done.1), channel_id=1, source_target_pairs={{0,2},{1,3},{2,0},{3,1},{4,6},{5,7},{6,4},{7,5},{8,10},{9,11},{10,... | collective-permute-start | bytes 3538952 | tf_op jit(solution)/shard_map/ppermute | solution.py:1627
  40.3 55.6 %collective-permute-start.7 = (bf16[1536,768]{1,0:T(8,128)(2,1)}, bf16[1536,768]{1,0:T(8,128)(2,1)}, u32[]{:S(2)}, u32[]{:S(2)}) collective-permute-start(bf16[1536,768]{1,0:T(8,128)(2,1)} %pack.5.refs_1_), channel_id=1, source_target_pairs={{0,1},{1,0},{2,3},{3,2},{4,5},{5,4},{6,7},{7,6},{8,9},{9,8},{10,11... | collective-permute-start | bytes 7077896 | tf_op jit(solution)/shard_map/ppermute | solution.py:1627
  40.5 77.3 %collective-permute-start.6 = (bf16[1536,768]{1,0:T(8,128)(2,1)}, bf16[1536,768]{1,0:T(8,128)(2,1)}, u32[]{:S(2)}, u32[]{:S(2)}) collective-permute-start(bf16[1536,768]{1,0:T(8,128)(2,1)} %pack.5.refs_1_), channel_id=1, source_target_pairs={{0,2},{1,3},{2,0},{3,1},{4,6},{5,7},{6,4},{7,5},{8,10},{9,11},{10,... | collective-permute-start | bytes 7077896 | tf_op jit(solution)/shard_map/ppermute | solution.py:1627
  41.6 25.9 %copy-start.15 = (s32[4]{0:T(128)S(1)}, s32[4]{0:T(128)}, u32[]{:S(2)}) copy-start(s32[4]{0:T(128)} %param.23) | copy-start | bytes 52
  41.6 26.6 %copy-start.12 = (bf16[768]{0:T(1024)(128)(2,1)S(1)}, bf16[768]{0:T(1024)(128)(2,1)}, u32[]{:S(2)}) copy-start(bf16[768]{0:T(1024)(128)(2,1)} %param.31) | copy-start | bytes 4612
  41.6 27.2 %copy-start.13 = (bf16[768]{0:T(1024)(128)(2,1)S(1)}, bf16[768]{0:T(1024)(128)(2,1)}, u32[]{:S(2)}) copy-start(bf16[768]{0:T(1024)(128)(2,1)} %param.36) | copy-start | bytes 4612
  41.6 27.8 %collective-permute-start.3 = (bf16[768,768]{1,0:T(8,128)(2,1)S(1)}, bf16[768,768]{1,0:T(8,128)(2,1)S(1)}, u32[]{:S(2)}, u32[]{:S(2)}) collective-permute-start(bf16[768,768]{1,0:T(8,128)(2,1)S(1)} %copy-done.1), channel_id=1, source_target_pairs={{0,1},{1,0},{2,3},{3,2},{4,5},{5,4},{6,7},{7,6},{8,9},{9,8},{10,11... | collective-permute-start | bytes 3538952 | tf_op jit(solution)/shard_map/ppermute | solution.py:1627
  41.9 1.1 copy-start.2
  67.5 1.9 copy-start.3
  67.5 3.0 collective-permute-start.5
  69.4 1.0 copy-start.4
  70.5 1.4 copy-start
  117.8 4.7 %collective-permute-start.8 = (bf16[1536,768]{1,0:T(8,128)(2,1)}, bf16[1536,768]{1,0:T(8,128)(2,1)S(1)}, u32[]{:S(2)}, u32[]{:S(2)}) collective-permute-start(bf16[1536,768]{1,0:T(8,128)(2,1)} %collective-permute-done.6.refs_1_), channel_id=1, source_target_pairs={{0,1},{1,0},{2,3},{3,2},{4,5},{5,4},{6,7},{7,6},{8,9},{9,8},{10,11... | collective-permute-start | bytes 7077896 | tf_op jit(solution)/shard_map/ppermute | solution.py:1627
  122.6 1.4 copy-start.6
  198.3 156.5 %all-to-all-start.1 = ((bf16[8,192,768]{2,1,0:T(8,128)(2,1)}), bf16[8,192,768]{2,1,0:T(8,128)(2,1)S(1)}, u32[]{:S(2)}, u32[]{:S(2)}) async-start(bf16[8,192,768]{2,1,0:T(8,128)(2,1)} %bitcast.31), calls=%async_computation.1 | async-start | bytes 4718592 | tf_op jit(solution)/shard_map/all_to_all | solution.py:1762
  349.0 5.2 %copy-start.10 = (f32[24,128]{1,0:T(8,128)S(1)}, f32[24,128]{1,0:T(8,128)}, u32[]{:S(2)}) copy-start(f32[24,128]{1,0:T(8,128)} %get-tuple-element.114) | copy-start | bytes 36868
  349.0 5.8 %copy-start.9 = (bf16[512,768]{1,0:T(8,128)(2,1)S(1)}, bf16[512,768]{1,0:T(8,128)(2,1)}, u32[]{:S(2)}) copy-start(bf16[512,768]{1,0:T(8,128)(2,1)} %get-tuple-element.149) | copy-start | bytes 2359300
  354.8 1.7 copy-start.7

commit v4 on v3

--- a/solution.py
+++ b/solution.py
@@ -23,8 +23,7 @@
 HEAD_BLOCK = 256
 BLOCK_HEADS = HEAD_BLOCK // HEAD_DIM
 Q_BLOCK = 256
-K_BLOCK = 512
-FORWARD_K_BLOCK = 256
+K_BLOCK = 256
 HIDDEN_BLOCK = 256
 MEMORY_BLOCK = 768
 FINISH_BLOCK = 384
@@ -478,7 +477,7 @@
         for which in range(2)
     ]
     ones = jnp.ones((TILE_ROWS, slots), BF16)
-    keys = spans(slots, FORWARD_K_BLOCK)
+    keys = spans(slots, K_BLOCK)
 
     def lanes_of(pair):
         return slice(pair * LANES, (pair + 1) * LANES)

time: 365 us -> 364 us (level)
  no operation moved by 1% of the time
where the time goes in v4:
time: 364 us; the launch traced here: 359 us
  Pallas kernels  291 us (80%)
  waiting for transfers between devices  33.8 us (9%)
  local copies, waits for them, and re-layouts  15.5 us (4%)
  starting transfers between devices  15.2 us (4%)
    pallas_call x6, Pallas kernels, call(): pl.pallas_call(kernel, grid=grid, in_specs=in_specs, out_specs=out_specs,...  167 us
    pallas_call x1, Pallas kernels, tail_sums(): pl.pallas_call(functools.partial(tail_kernel, size, peers, buckets, heads...  111 us
    ppermute x9, waiting for transfers between devices, swap(): return lax.ppermute(array, 'mp', [(i, i ^ bit) for i in range(size)])  33.8 us
    unnamed x36, local copies, waits for them, and re-layouts  10.5 us
    pallas_call x3, Pallas kernels, pack(): pl.pallas_call(functools.partial(pack_kernel, flipped), out_shape=shape((...  8.23 us
    all_to_all x1, starting transfers between devices, shards(): lax.all_to_all(memory_rows.reshape(dp_size, slots // dp_size, features),...  7.41 us
  transfers between devices with their start and end apart: 11, of which 6 were waited for; matrix products, arithmetic and copies ran while one was open for 2% of the time, Pallas kernels for 60%

profile of v4, /device:TPU:0, one launch (start us, length us, event | category | flops | bytes accessed | tf_op | source)
XLA Modules:
  0.0 359.0 jit_solution(6048967043845285523)
XLA Ops:
  0.7 2.3 pack.3.refs_2_.refs_12_
  3.0 7.4 %all-to-all-start = ((bf16[8,192,768]{2,1,0:T(8,128)(2,1)}), bf16[8,192,768]{2,1,0:T(8,128)(2,1)S(1)}, u32[]{:S(2)}, u32[]{:S(2)}) async-start(bf16[8,192,768]{2,1,0:T(8,128)(2,1)} %bitcast.30), calls=%async_computation | async-start | bytes 4718592 | tf_op jit(solution)/shard_map/all_to_all | solution.py:1706
  10.4 1.6 collective-permute-start.1
  12.0 1.3 copy.37
  13.9 3.4 pack.5.refs_1_
  17.3 2.5 pack.4.refs_2_.refs_12_
  19.8 0.7 iota_compare_fusion.1
  20.5 1.1 bitcast_select_fusion.ids_ref.refs_7_
  21.7 17.1 %collective-permute-done.1.refs_3_.refs_13_ = bf16[784,768]{1,0:T(8,128)(2,1)} collective-permute-done((bf16[784,768]{1,0:T(8,128)(2,1)}, bf16[784,768]{1,0:T(8,128)(2,1)}, u32[]{:S(2)}, u32[]{:S(2)}) %collective-permute-start.1) | collective-permute-done | bytes 1204256 | tf_op jit(solution)/shard_map/ppermute | solution.py:1626
  38.8 1.5 collective-permute-start.4
  41.9 1.1 copy-done.2
  42.9 17.7 %self_forward.1 = (bf16[512,768]{1,0:T(8,128)(2,1)}, bf16[512,768]{1,0:T(8,128)(2,1)}, bf16[512,768]{1,0:T(8,128)(2,1)}, bf16[512,768]{1,0:T(8,128)(2,1)}, f32[3...) custom-call(bf16[512,768]{1,0:T(8,128)(2,1)} %refs_0_.3, f32[1,768]{1,0:T(1,128)} %reshape.66.gain_ref.refs_1_, ...), custom_call_target="tpu_custom_call" | custom-call | flops 1048576 | bytes 65536 | tf_op jit(solution)/shard_map/self_forward/pallas_call | solution.py:959
  60.6 6.9 %collective-permute-done.4.refs_3_.refs_13_ = bf16[768,768]{1,0:T(8,128)(2,1)S(1)} collective-permute-done((bf16[768,768]{1,0:T(8,128)(2,1)S(1)}, bf16[768,768]{1,0:T(8,128)(2,1)S(1)}, u32[]{:S(2)}, u32[]{:S(2)}) %collective-permute-start.4) | collective-permute-done | bytes 1179680 | tf_op jit(solution)/shard_map/ppermute | solution.py:1626
  67.5 0.7 dynamic_slice.8.length_ref
  69.4 1.0 copy-done.4
  70.5 1.4 copy-done
  71.9 24.0 %cross_forward.1 = (bf16[512,768]{1,0:T(8,128)(2,1)}, bf16[1536,768]{1,0:T(8,128)(2,1)}, bf16[1536,768]{1,0:T(8,128)(2,1)}, bf16[512,768]{1,0:T(8,128)(2,1)}, f32[3,8,512]{2,1,0:T(8,128)}, /*index=5*/f32[512,768]{1,0:T(8,128)}) custom-call(s32[1]{0:T(128)} %dynamic_slice.8.length_ref, f32[512,768]{1,0:T(8,128)} %get-tuple-element.74.rows_ref.refs_5_, ...), custom_call_target="tpu_custom_call" | custom-call | flops 1048576 | bytes 65536 | tf_op jit(solution)/shard_map/cross_forward/pallas_call | solution.py:959
  95.9 17.1 %feed_forward.2 = (bf16[768,768]{1,0:T(8,128)(2,1)}, bf16[768,768]{1,0:T(8,128)(2,1)}, f32[512,768]{1,0:T(8,128)}, f32[512,768]{1,0:T(8,128)}) custom-call(f32[512,768]{1,0:T(8,128)} %get-tuple-element.77.rows_ref, f32[1,768]{1,0:T(1,128)} %reshape.68.gain_ref, bf16[512,768]{1,0:T(8,128)(2,1)} %cotangent_ref.3, ...), custom_call_target="tpu_custom_call" | custom-call | flops 1048576 | bytes 65536 | tf_op jit(solution)/shard_map/feed_forward/pallas_call | solution.py:959
  113.0 4.8 %collective-permute-done.6.refs_1_ = bf16[1536,768]{1,0:T(8,128)(2,1)} collective-permute-done((bf16[1536,768]{1,0:T(8,128)(2,1)}, bf16[1536,768]{1,0:T(8,128)(2,1)}, u32[]{:S(2)}, u32[]{:S(2)}) %collective-permute-start.6) | collective-permute-done | bytes 2359328 | tf_op jit(solution)/shard_map/ppermute | solution.py:1626
  117.8 4.7 %collective-permute-done.8.refs_0_ = bf16[1536,768]{1,0:T(8,128)(2,1)S(1)} collective-permute-done((bf16[1536,768]{1,0:T(8,128)(2,1)}, bf16[1536,768]{1,0:T(8,128)(2,1)S(1)}, u32[]{:S(2)}, u32[]{:S(2)}) %collective-permute-start.8) | collective-permute-done | bytes 2359328 | tf_op jit(solution)/shard_map/ppermute | solution.py:1626
  122.6 1.4 copy-done.6
  124.0 17.6 %feed_forward.3 = (bf16[768,768]{1,0:T(8,128)(2,1)}, bf16[768,768]{1,0:T(8,128)(2,1)}, bf16[512,768]{1,0:T(8,128)(2,1)}, f32[512,768]{1,0:T(8,128)}, bf16[512,768]{1,0:T(8,128)(2,1)}, /*index=5*/f32[8,768]{1,0:T(8,128)}) custom-call(f32[512,768]{1,0:T(8,128)} %get-tuple-element.77.rows_ref, f32[1,768]{1,0:T(1,128)} %reshape.68.gain_ref, ...), custom_call_target="tpu_custom_call" | custom-call | flops 1048576 | bytes 65536 | tf_op jit(solution)/shard_map/feed_forward/pallas_call | solution.py:959
  141.5 56.2 %cross_backward.1 = (bf16[768,768]{1,0:T(8,128)(2,1)}, bf16[2,48,768]{2,1,0:T(8,128)(2,1)}, bf16[768,768]{1,0:T(8,128)(2,1)}, bf16[768,768]{1,0:T(8,128)(2,1)}, ...) custom-call(s32[1]{0:T(128)} %dynamic_slice.8.length_ref, ...), custom_call_target="tpu_custom_call" | custom-call | flops 1048576 | bytes 65536 | tf_op jit(solution)/shard_map/cross_backward/pallas_call | solution.py:959
  197.7 3.9 %all-to-all-start.1 = ((bf16[8,192,768]{2,1,0:T(8,128)(2,1)}), bf16[8,192,768]{2,1,0:T(8,128)(2,1)S(1)}, u32[]{:S(2)}, u32[]{:S(2)}) async-start(bf16[8,192,768]{2,1,0:T(8,128)(2,1)} %bitcast.31), calls=%async_computation.1 | async-start | bytes 4718592 | tf_op jit(solution)/shard_map/all_to_all | solution.py:1761
  201.6 34.6 %self_backward.1 = (bf16[768,768]{1,0:T(8,128)(2,1)}, bf16[768,768]{1,0:T(8,128)(2,1)}, bf16[768,768]{1,0:T(8,128)(2,1)}, bf16[12,512,512]{2,1,0:T(8,128)(2,1)}, f32[512,768]{1,0:T(8,128)}, /*index=5*/f32[8,768]{1,0:T(8,128)}) custom-call(bf16[512,768]{1,0:T(8,128)(2,1)} %refs_0_.3, f32[1,768]{1,0:T(1,128)} %reshape.66.gain_ref.refs_1_, ...), custom_call_target="tpu_custom_call" | custom-call | flops 1048576 | bytes 65536 | tf_op jit(solution)/shard_map/self_backward/pallas_call | solution.py:959
  236.3 110.8 %tail_sums.1 = (bf16[768,768]{1,0:T(8,128)(2,1)}, bf16[768,768]{1,0:T(8,128)(2,1)}, bf16[768,768]{1,0:T(8,128)(2,1)}, bf16[768,768]{1,0:T(8,128)(2,1)}, f32[24,128]{1,0:T(8,128)}) custom-call(bf16[2,48,768]{2,1,0:T(8,128)(2,1)} %get-tuple-element.103.refs_0_, bf16[768,768]{1,0:T(8,128)(2,1)} %get-tuple-element.104.refs_1_, ...), custom_call_target="tpu_custom_call" | custom-call | flops 1048576 | bytes 65536 | tf_op jit(solution)/shard_map/tail_sums/pallas_call | solution.py:1585
  347.1 0.7 slice_reduce_fusion
  348.4 5.2 %finish.1 = (f32[768,768]{1,0:T(8,128)}, f32[768,768]{1,0:T(8,128)}, f32[192,768]{1,0:T(8,128)}, f32[192,768]{1,0:T(8,128)}, f32[192,768]{1,0:T(8,128)}, /*index...) custom-call(bf16[768,768]{1,0:T(8,128)(2,1)} %get-tuple-element.115.refs_, ...), custom_call_target="tpu_custom_call" | custom-call | flops 1048576 | bytes 65536 | tf_op jit(solution)/shard_map/finish/pallas_call | solution.py:1229
  354.2 0.9 copy.41
  355.1 0.8 copy-done.7
  355.9 1.1 copy.42
  357.1 1.4 copy.43
  (47 shorter events, 4.7 us)
Async XLA Ops:
  3.0 9.0 %copy-start.8 = (s32[512,512]{1,0:T(8,128)S(1)}, s32[512,512]{1,0:T(8,128)}, u32[]{:S(2)}) copy-start(s32[512,512]{1,0:T(8,128)} %param.24) | copy-start | bytes 3145732
  3.0 67.5 %all-to-all-start = ((bf16[8,192,768]{2,1,0:T(8,128)(2,1)}), bf16[8,192,768]{2,1,0:T(8,128)(2,1)S(1)}, u32[]{:S(2)}, u32[]{:S(2)}) async-start(bf16[8,192,768]{2,1,0:T(8,128)(2,1)} %bitcast.30), calls=%async_computation | async-start | bytes 4718592 | tf_op jit(solution)/shard_map/all_to_all | solution.py:1706
  10.4 2.9 copy-start.14
  10.4 28.3 %collective-permute-start.1 = (bf16[784,768]{1,0:T(8,128)(2,1)}, bf16[784,768]{1,0:T(8,128)(2,1)}, u32[]{:S(2)}, u32[]{:S(2)}) collective-permute-start(bf16[784,768]{1,0:T(8,128)(2,1)} %pack.3.refs_2_.refs_12_), channel_id=1, source_target_pairs={{0,2},{1,3},{2,0},{3,1},{4,6},{5,7},{6,4},{7,5},{8,10},{9,11},{10,... | collective-permute-start | bytes 3612680 | tf_op jit(solution)/shard_map/ppermute | solution.py:1626
  12.0 29.6 %collective-permute-start = (bf16[784,768]{1,0:T(8,128)(2,1)}, bf16[784,768]{1,0:T(8,128)(2,1)}, u32[]{:S(2)}, u32[]{:S(2)}) collective-permute-start(bf16[784,768]{1,0:T(8,128)(2,1)} %pack.3.refs_2_.refs_12_), channel_id=1, source_target_pairs={{0,1},{1,0},{2,3},{3,2},{4,5},{5,4},{6,7},{7,6},{8,9},{9,8},{10,11... | collective-permute-start | bytes 3612680 | tf_op jit(solution)/shard_map/ppermute | solution.py:1626
  17.3 3.2 copy-start.5
  19.8 19.0 %copy-start.1 = (bf16[768,768]{1,0:T(8,128)(2,1)S(1)}, bf16[768,768]{1,0:T(8,128)(2,1)}, u32[]{:S(2)}) copy-start(bf16[768,768]{1,0:T(8,128)(2,1)} %pack.4.refs_2_.refs_12_) | copy-start | bytes 3538948
  19.8 21.3 %copy-start.11 = (bf16[768]{0:T(1024)(128)(2,1)S(1)}, bf16[768]{0:T(1024)(128)(2,1)}, u32[]{:S(2)}) copy-start(bf16[768]{0:T(1024)(128)(2,1)} %param.26) | copy-start | bytes 4612
  38.8 3.1 collective-permute-start.2
  38.8 28.8 %collective-permute-start.4 = (bf16[768,768]{1,0:T(8,128)(2,1)S(1)}, bf16[768,768]{1,0:T(8,128)(2,1)S(1)}, u32[]{:S(2)}, u32[]{:S(2)}) collective-permute-start(bf16[768,768]{1,0:T(8,128)(2,1)S(1)} %copy-done.1), channel_id=1, source_target_pairs={{0,2},{1,3},{2,0},{3,1},{4,6},{5,7},{6,4},{7,5},{8,10},{9,11},{10,... | collective-permute-start | bytes 3538952 | tf_op jit(solution)/shard_map/ppermute | solution.py:1626
  40.3 55.7 %collective-permute-start.7 = (bf16[1536,768]{1,0:T(8,128)(2,1)}, bf16[1536,768]{1,0:T(8,128)(2,1)}, u32[]{:S(2)}, u32[]{:S(2)}) collective-permute-start(bf16[1536,768]{1,0:T(8,128)(2,1)} %pack.5.refs_1_), channel_id=1, source_target_pairs={{0,1},{1,0},{2,3},{3,2},{4,5},{5,4},{6,7},{7,6},{8,9},{9,8},{10,11... | collective-permute-start | bytes 7077896 | tf_op jit(solution)/shard_map/ppermute | solution.py:1626
  40.5 77.3 %collective-permute-start.6 = (bf16[1536,768]{1,0:T(8,128)(2,1)}, bf16[1536,768]{1,0:T(8,128)(2,1)}, u32[]{:S(2)}, u32[]{:S(2)}) collective-permute-start(bf16[1536,768]{1,0:T(8,128)(2,1)} %pack.5.refs_1_), channel_id=1, source_target_pairs={{0,2},{1,3},{2,0},{3,1},{4,6},{5,7},{6,4},{7,5},{8,10},{9,11},{10,... | collective-permute-start | bytes 7077896 | tf_op jit(solution)/shard_map/ppermute | solution.py:1626
  41.6 25.9 %copy-start.15 = (s32[4]{0:T(128)S(1)}, s32[4]{0:T(128)}, u32[]{:S(2)}) copy-start(s32[4]{0:T(128)} %param.23) | copy-start | bytes 52
  41.6 26.6 %copy-start.12 = (bf16[768]{0:T(1024)(128)(2,1)S(1)}, bf16[768]{0:T(1024)(128)(2,1)}, u32[]{:S(2)}) copy-start(bf16[768]{0:T(1024)(128)(2,1)} %param.31) | copy-start | bytes 4612
  41.6 27.2 %copy-start.13 = (bf16[768]{0:T(1024)(128)(2,1)S(1)}, bf16[768]{0:T(1024)(128)(2,1)}, u32[]{:S(2)}) copy-start(bf16[768]{0:T(1024)(128)(2,1)} %param.36) | copy-start | bytes 4612
  41.6 27.8 %collective-permute-start.3 = (bf16[768,768]{1,0:T(8,128)(2,1)S(1)}, bf16[768,768]{1,0:T(8,128)(2,1)S(1)}, u32[]{:S(2)}, u32[]{:S(2)}) collective-permute-start(bf16[768,768]{1,0:T(8,128)(2,1)S(1)} %copy-done.1), channel_id=1, source_target_pairs={{0,1},{1,0},{2,3},{3,2},{4,5},{5,4},{6,7},{7,6},{8,9},{9,8},{10,11... | collective-permute-start | bytes 3538952 | tf_op jit(solution)/shard_map/ppermute | solution.py:1626
  41.9 1.1 copy-start.2
  67.5 1.9 copy-start.3
  67.5 3.0 collective-permute-start.5
  69.4 1.0 copy-start.4
  70.5 1.4 copy-start
  117.8 4.7 %collective-permute-start.8 = (bf16[1536,768]{1,0:T(8,128)(2,1)}, bf16[1536,768]{1,0:T(8,128)(2,1)S(1)}, u32[]{:S(2)}, u32[]{:S(2)}) collective-permute-start(bf16[1536,768]{1,0:T(8,128)(2,1)} %collective-permute-done.6.refs_1_), channel_id=1, source_target_pairs={{0,1},{1,0},{2,3},{3,2},{4,5},{5,4},{6,7},{7,6},{8,9},{9,8},{10,11... | collective-permute-start | bytes 7077896 | tf_op jit(solution)/shard_map/ppermute | solution.py:1626
  122.6 1.4 copy-start.6
  197.7 156.5 %all-to-all-start.1 = ((bf16[8,192,768]{2,1,0:T(8,128)(2,1)}), bf16[8,192,768]{2,1,0:T(8,128)(2,1)S(1)}, u32[]{:S(2)}, u32[]{:S(2)}) async-start(bf16[8,192,768]{2,1,0:T(8,128)(2,1)} %bitcast.31), calls=%async_computation.1 | async-start | bytes 4718592 | tf_op jit(solution)/shard_map/all_to_all | solution.py:1761
  348.4 5.2 %copy-start.10 = (f32[24,128]{1,0:T(8,128)S(1)}, f32[24,128]{1,0:T(8,128)}, u32[]{:S(2)}) copy-start(f32[24,128]{1,0:T(8,128)} %get-tuple-element.114) | copy-start | bytes 36868
  348.4 5.8 %copy-start.9 = (bf16[512,768]{1,0:T(8,128)(2,1)S(1)}, bf16[512,768]{1,0:T(8,128)(2,1)}, u32[]{:S(2)}) copy-start(bf16[512,768]{1,0:T(8,128)(2,1)} %get-tuple-element.149) | copy-start | bytes 2359300
  354.2 1.7 copy-start.7
